TPU v7x, 32 devices: a whole 2x2x4 slice. The times are simulated.
32 devices in a mesh: scene: 16 (over z, y, core), frame: 2 (over x).
Axes of the slice: x: 2, y: 2, z: 4, core: 2. Of those that a mesh axis runs over, the one named last changes fastest.
Arguments:
- tokens: bfloat16 [4096, 1024], P(('scene', 'frame')), may hold values from -6 to 6
- cotangent: bfloat16 [4096, 1024], P(('scene', 'frame')), may hold values from -6 to 6
- scene_ids: int32 [4096], P(('scene', 'frame')), may hold values from 0 to 63, as said below
- frame_index: int32 [4096], P(('scene', 'frame')), may hold values from 0 to 3, as said below
- qkv_weight: bfloat16 [2, 1024, 3072], P(None, ('scene', 'frame')), may hold values from -0.1875 to 0.1875
- qkv_bias: bfloat16 [2, 3072], P(None, ('scene', 'frame')), may hold values from -1.796875 to 1.796875
- proj_weight: bfloat16 [2, 1024, 1024], P(None, ('scene', 'frame')), may hold values from -2 to 2
- fc1_weight: bfloat16 [2, 1024, 4096], P(None, ('scene', 'frame')), may hold values from -0.1875 to 0.1875
- fc1_bias: bfloat16 [2, 4096], P(None, ('scene', 'frame')), may hold values from -1.796875 to 1.796875
- fc2_weight: bfloat16 [2, 4096, 1024], P(None, ('scene', 'frame')), may hold values from -0.09375 to 0.09375
- out_bias: bfloat16 [2, 2, 1024], P(None, None, ('scene', 'frame')), may hold values from -1.796875 to 1.796875
- norm_gain: bfloat16 [2, 2, 1024], P(None, None, ('scene', 'frame')), may hold values from 0.5 to 1.5
- norm_bias: bfloat16 [2, 2, 1024], P(None, None, ('scene', 'frame')), may hold values from -1.796875 to 1.796875
- layer_scale: bfloat16 [2, 2, 1024], P(None, None, ('scene', 'frame')), may hold values from 0.29882812 to 1
- qk_gain: bfloat16 [2, 2, 64], replicated, may hold values from 0.5 to 1.5
- qk_bias: bfloat16 [2, 2, 64], replicated, may hold values from -1.796875 to 1.796875
Outputs:
- activations: bfloat16 [4096, 1024], P(('scene', 'frame'))
- input_grad: bfloat16 [4096, 1024], P(('scene', 'frame'))
- qkv_weight_grad: float32 [2, 1024, 3072], P(None, ('scene', 'frame'))
- qkv_bias_grad: float32 [2, 3072], P(None, ('scene', 'frame'))
- proj_weight_grad: float32 [2, 1024, 1024], P(None, ('scene', 'frame'))
- fc1_weight_grad: float32 [2, 1024, 4096], P(None, ('scene', 'frame'))
- fc1_bias_grad: float32 [2, 4096], P(None, ('scene', 'frame'))
- fc2_weight_grad: float32 [2, 4096, 1024], P(None, ('scene', 'frame'))
- out_bias_grad: float32 [2, 2, 1024], P(None, None, ('scene', 'frame'))
- norm_gain_grad: float32 [2, 2, 1024], P(None, None, ('scene', 'frame'))
- norm_bias_grad: float32 [2, 2, 1024], P(None, None, ('scene', 'frame'))
- layer_scale_grad: float32 [2, 2, 1024], P(None, None, ('scene', 'frame'))
- qk_gain_grad: float32 [2, 2, 64], replicated
- qk_bias_grad: float32 [2, 2, 64], replicated
Inputs may be any that keep to these rules, and one draw needn't show every extreme that they name: `scene_ids`: tokens of one scene are whole consecutive frames of 64 tokens within the tokens of one index of scene; a scene's id is the number of its first frame among all frames; index 0 of scene holds a single scene; the last frame of the last index of scene is a scene of its own. `frame_index`: the frame's position within its scene, counted from 0, equal for the 64 tokens of one frame.
All inputs are finite; a program needn't handle non-finite values.
Results may differ from a plain program's by a relative error of at most 0.014.
Values may be sent and summed in bfloat16 or wider, within the bound.
No kernel may reach another device: no remote copies, remote signals or barrier semaphores. Data moves between devices by JAX's collectives and lax.ppermute only.
A program may use at most 320 MiB of HBM per device.

v0:
```python
import jax
import jax.numpy as jnp
import numpy as np
from jax import lax
from jax.experimental import pallas as pl
from jax.experimental.pallas import tpu as pltpu
from jax.sharding import Mesh
from jax.sharding import PartitionSpec as P

EPSILON = 1e-06
FRAME_TOK = 64
LOW = jnp.bfloat16
WIDE = jnp.float32
EVERY = ("outer", "inner", "core", "frame")
REST = ("outer", "inner")
TEAM = ("core", "frame")
ROOT_HALF = 0.7071067811865476
ROOT_TWO_PI = 0.3989422804014327
MEBI = 1024 * 1024
OUT, GAIN, SHIFT, SCALE = 0, 4, 8, 12
HOPS = (0, 0, 1, 0, 1, 0, 1, 0) + (1, 0, 1, 1, 0, 0, 1, 0)
LEAD = (4, 4)


def dot(left, right):
    return jnp.dot(left, right, preferred_element_type=WIDE)


def dot_tn(left, right):
    return lax.dot_general(left, right, (((0,), (0,)), ((), ())), preferred_element_type=WIDE)


def dot_nt(left, right):
    return lax.dot_general(left, right, (((1,), (1,)), ((), ())), preferred_element_type=WIDE)


def normed(values):
    center = values - jnp.mean(values, axis=-1, keepdims=True)
    rate = lax.rsqrt(jnp.mean(center * center, axis=-1, keepdims=True) + EPSILON)
    return center * rate, rate


def normed_back(grad, unit, rate, gain):
    inner = grad * gain
    mean_one = jnp.mean(inner, axis=-1, keepdims=True)
    mean_two = jnp.mean(inner * unit, axis=-1, keepdims=True)
    return rate * (inner - mean_one - unit * mean_two)


def shape_of(shape, dtype):
    return jax.ShapeDtypeStruct(shape, dtype)


def call(kernel, outs, args, name, flops=0, scratch=(), scalars=0, far_in=(), far_out=()):
    hbm = pl.BlockSpec(memory_space=pltpu.HBM)
    vmem = pl.BlockSpec(memory_space=pltpu.VMEM)
    smem = pl.BlockSpec(memory_space=pltpu.SMEM)
    in_specs = [smem if i < scalars else hbm if i in far_in else vmem for i in range(len(args))]
    bytes_all = sum(m.size * m.dtype.itemsize for m in args)
    bytes_all += sum(int(np.prod(s.shape)) * s.dtype.itemsize for s in outs)
    sized = [s for s in scratch if hasattr(s, "shape") and s.memory_space == pltpu.VMEM]
    held = sum(int(np.prod(s.shape)) * s.dtype.itemsize for s in sized)
    limit = (held * 5 // 4 + bytes_all * 2 // 5 if flops else bytes_all) + (8 if flops else 3) * MEBI
    args = [pltpu.with_memory_space_constraint(m, pltpu.HBM) if i in far_in else m for i, m in enumerate(args)]
    outs = [pltpu.HBM(m.shape, m.dtype) if i in far_out else m for i, m in enumerate(outs)]
    return pl.pallas_call(
        kernel,
        out_shape=list(outs),
        in_specs=in_specs,
        out_specs=[hbm if i in far_out else vmem for i in range(len(outs))],
        scratch_shapes=list(scratch),
        compiler_params=pltpu.CompilerParams(vmem_limit_bytes=limit),
        cost_estimate=pl.CostEstimate(flops=flops, bytes_accessed=bytes_all, transcendentals=0),
        name=name,
    )(*args)


def swap(values, axis):
    return lax.ppermute(values, axis, [(0, 1), (1, 0)])


def cross(values):
    return lax.ppermute(values, TEAM, [(0, 3), (1, 2), (2, 1), (3, 0)])


def team_gather(values, work=None, pump=None):
    if lax.axis_size("frame") == 2:
        far = swap(values, "frame")
        near = swap(work(values) if work else values, "core")
        far = pump(far) if pump else far
        return [values, far, near, swap(far, "core")]
    both = lax.all_gather(values, "frame", axis=0, tiled=True)
    return [both, swap(both, "core")]


def team_sum(own, peer, work=None, pump=None):
    if lax.axis_size("frame") == 2:
        far = own[1] + swap(peer[1], "core").astype(WIDE)
        came = swap(far.astype(LOW), "frame")
        near = swap(work(peer[0]) if work else peer[0], "core")
        came = pump(came) if pump else came
        return [own[0], near, came]
    total = own[0] + swap(peer[0], "core").astype(WIDE)
    return [lax.psum_scatter(total.astype(LOW), "frame", scatter_dimension=0, tiled=True).astype(WIDE)]


def exchange_columns(values):
    parts = values.transpose(1, 0, 2)
    frames = lax.axis_size("frame")
    parts = parts.reshape((2, frames) + parts.shape[1:])
    both = lax.all_to_all(parts, "frame", 1, 1, tiled=True)
    here = lax.axis_index("core")
    keep = lax.dynamic_index_in_dim(both, here, 0, keepdims=False)
    came = swap(lax.dynamic_index_in_dim(both, 1 - here, 0, keepdims=False), "core")
    out = jnp.stack([jnp.where(here == 0, keep, came), jnp.where(here == 0, came, keep)], axis=0)
    return out.reshape((2 * frames,) + out.shape[2:])


SMALL_ROWS = 16


def split_weights(depth, weights, vectors, part, rest, me):
    qkv, up = weights
    _, rows, width = qkv.shape
    width //= 3
    hidden = up.shape[2] // 4
    lanes = hidden // rest
    extra = SMALL_ROWS if vectors else 0

    far = list(vectors)

    def kernel(me_ref, qkv_ref, up_ref, *refs):
        outs, small = refs[len(far) : len(far) + 4], refs[len(far) + 4 : -1]
        copies = []
        for source, target in zip(refs, small):
            copies.append(pltpu.make_async_copy(source, target, refs[-1].at[len(copies)]))
            copies[-1].start()
        wait_all(copies)
        for away, out in enumerate(outs):
            member = jnp.bitwise_xor(me_ref[0], away)
            for s in range(3):
                start = pl.multiple_of(s * width + member * part, 128)
                out[:rows, s * part : (s + 1) * part] = qkv_ref[depth, :, pl.ds(start, part)]
            for f in range(rest):
                start = pl.multiple_of((f * 4 + member) * lanes, 128)
                at = 3 * part + f * lanes
                out[:rows, at : at + lanes] = up_ref[depth, :, pl.ds(start, lanes)]
            if not vectors:
                continue
            out[rows:, :] = jnp.zeros((extra, out.shape[1]), LOW)
            bias_qkv, bias_up, ids = small[:3]
            for i, ref in enumerate(small[3:]):
                for d in range(2):
                    for j in range(2):
                        at = rows + 4 * i + 2 * d + j
                        out[at : at + 1, : ref.shape[2]] = ref[d, j : j + 1, :]
            out[rows : rows + 2, 128 : 128 + bias_qkv.shape[1]] = bias_qkv[...]
            out[rows : rows + 2, 256 : 256 + bias_up.shape[1]] = bias_up[...]
            out[rows : rows + 1, 512 : 512 + ids.shape[1]] = ids[...].astype(WIDE).astype(LOW)

    out = shape_of((rows + extra, 3 * part + hidden), qkv.dtype)
    scratch = [pltpu.VMEM(m.shape, m.dtype) for m in far] + [pltpu.SemaphoreType.DMA((len(far) + 1,))]
    args = [me, qkv, up, *far]
    return call(kernel, [out] * 4, args, "split_weights", 0, scratch, 1, far_in=range(3, 3 + len(far)))


def pack_weights(pieces, proj, down, depth, part, me, vectors):
    rows = proj.shape[1]
    unit = 4 * rows
    hidden = pieces[0].shape[1] - 3 * part

    def kernel(me_ref, p0, p1, p2, p3, proj_ref, down_ref, attn, up, small):
        for away, ref in enumerate((p0, p1, p2, p3)):
            member = jnp.bitwise_xor(me_ref[0], away)
            start = pl.multiple_of(member * rows, rows)
            attn[pl.ds(start, rows), : 3 * part] = ref[:rows, : 3 * part]
            up[pl.ds(start, rows), :] = ref[:rows, 3 * part :]
            if vectors:
                small[member] = ref[rows:, :640]
        for j in range(4):
            attn[j * rows : (j + 1) * rows, 3 * part :] = proj_ref[depth, :, j * part : (j + 1) * part]
        up[unit:, :] = down_ref[depth]
        if vectors:
            attn[unit:, :] = jnp.zeros((SMALL_ROWS, 4 * part), LOW)
            for at, start, size in ((0, 0, 32), (128, 128, 96), (512, 256, 128)):
                joined = [small[m, :, start : start + size].astype(WIDE) for m in range(4)]
                value = jnp.concatenate(joined, axis=1).astype(LOW)
                attn[unit:, at : at + 4 * size] = value

    extra = SMALL_ROWS if vectors else 0
    outs = [shape_of((unit + extra, 4 * part), LOW), shape_of((2 * unit, hidden), LOW)]
    scratch = [pltpu.VMEM((4, SMALL_ROWS, 640), LOW)]
    return call(kernel, outs, [me, *pieces, proj, down], "pack_weights", scratch=scratch, scalars=1)


def unpack_vectors(source, table, me):
    rest, _, width = source.shape
    part = width // 4

    def kernel(me_ref, table_ref, *refs):
        vec, bias_qkv, bias_up, small, whole, semaphores = refs[source.count :]
        wait_all(source.start(refs[: source.count], table_ref, small, semaphores))
        for f in range(rest):
            vec[:, f * 128 : (f + 1) * 128] = small[f, :, :128].astype(WIDE)
            whole[:, f * 384 : (f + 1) * 384] = small[f, :, 128:512].astype(WIDE)
            start = pl.multiple_of(512 + me_ref[0] * 128, 128)
            bias_up[:, f * 128 : (f + 1) * 128] = small[f, :, pl.ds(start, 128)].astype(WIDE)
        for s in range(3):
            start = pl.multiple_of(s * width + me_ref[0] * part, 128)
            bias_qkv[:, s * part : (s + 1) * part] = whole[:, pl.ds(start, part)]

    outs = [shape_of((16, width), WIDE), shape_of((16, 3 * part), WIDE), shape_of((16, width), WIDE)]
    scratch = [
        pltpu.VMEM((rest, SMALL_ROWS, width), LOW),
        pltpu.VMEM((16, 3 * width), WIDE),
        pltpu.SemaphoreType.DMA((source.count,)),
    ]
    args = [me, table, *source.args]
    return call(kernel, outs, args, "unpack_vectors", 0, scratch, 2, far_in=range(2, 2 + source.count))


def spread(count, team):
    rest = count // team
    return [(i, (i % rest) * team + i // rest) for i in range(count)]


def widen(rows, width):
    height, columns = rows.shape
    parts = columns // width
    if parts == 1:
        return rows
    return rows.reshape(height, parts, width).transpose(1, 0, 2).reshape(parts * height, width)


def narrow(stacked, height):
    lead = stacked.shape[:-2]
    parts = stacked.shape[-2] // height
    if parts == 1:
        return stacked
    width = stacked.shape[-1]
    shaped = stacked.reshape(lead + (parts, height, width))
    return jnp.moveaxis(shaped, -3, -2).reshape(lead + (height, parts * width))


def ring_order(outer, inner):
    order = []
    for a in range(outer):
        row = range(1, inner) if a % 2 == 0 else range(inner - 1, 0, -1)
        order += [a * inner + b for b in row]
    return order + [a * inner for a in range(outer - 1, -1, -1)]


def ring_table():
    outer, inner = lax.axis_size("outer"), lax.axis_size("inner")
    order = ring_order(outer, inner)
    rest = outer * inner
    place = {team: i for i, team in enumerate(order)}
    table = np.array(
        [
            [[order[(place[f] + sign * k) % rest] for k in range(rest)] for sign in (-1, 1)]
            for f in range(rest)
        ],
        np.int32,
    )
    here = lax.axis_index("outer") * inner + lax.axis_index("inner")
    return lax.dynamic_index_in_dim(jnp.asarray(table), here, 0, keepdims=False)


def ring_shift(values, sign):
    order = ring_order(lax.axis_size("outer"), lax.axis_size("inner"))
    rest = len(order)
    return lax.ppermute(values, REST, [(order[i], order[(i + sign) % rest]) for i in range(rest)])


def ring_step(low_half, high_half):
    low_half, high_half = ring_shift(low_half, 1), ring_shift(high_half, -1)
    return lax.optimization_barrier((low_half, high_half))


class RingGather:
    def __init__(self, shard, cut, rest):
        self.steps = rest // 2
        self.cut = cut
        self.back, self.ahead = [shard], [shard]
        self.came = (ring_shift(shard, 1), ring_shift(shard, -1))

    def take(self, came):
        self.back.append(came[0])
        self.ahead.append(came[1])
        self.came = None
        if len(self.back) == self.steps:
            came = (came[0][: self.cut], came[1][self.cut :])
        if len(self.back) <= self.steps:
            self.came = (ring_shift(came[0], 1), ring_shift(came[1], -1))

    def rows(self, first, count):
        out = []
        for side, arrays in enumerate((self.back, self.ahead)):
            out += [(m, side, k, 0, first, count) for k, m in enumerate(arrays[: self.steps]) if k or not side]
        stop = min(first + count, self.cut)
        if stop > first:
            out.append((self.back[self.steps], 0, self.steps, 0, first, stop - first))
        start = max(first, self.cut)
        if start < first + count:
            out.append(
                (self.ahead[self.steps], 1, self.steps, start - first, start - self.cut, first + count - start)
            )
        return Pieces(out, 2 * self.steps, count)


def steps(count, ring):
    came = ()
    for _ in range(count):
        if ring.came is None:
            break
        came = tie(*ring.came)
        ring.take(came)
    return came


class Pieces:
    def __init__(self, entries, rest, rows):
        self.entries = entries
        self.args = [entry[0] for entry in entries]
        self.count = len(entries)
        self.shape = (rest, rows, self.args[0].shape[1])

    def start(self, refs, table_ref, target, semaphores):
        copies = []
        for ref, (_, side, k, first, begin, rows) in zip(refs, self.entries):
            spot = target.at[table_ref[side, k], pl.ds(first, rows), :]
            copies.append(pltpu.make_async_copy(ref.at[pl.ds(begin, rows), :], spot, semaphores.at[len(copies)]))
            copies[-1].start()
        return copies


class Whole:
    count = 1

    def __init__(self, array, first, rows):
        self.first = first
        self.args = [array]
        self.shape = (array.shape[0], rows, array.shape[2])

    def start(self, refs, table_ref, target, semaphores):
        source = refs[0].at[:, pl.ds(self.first, self.shape[1]), :]
        copy = pltpu.make_async_copy(source, target, semaphores.at[0])
        copy.start()
        return [copy]


def wait_all(copies):
    for copy in copies:
        copy.wait()


def tie(*values):
    return lax.optimization_barrier(values)


class RingSums:
    def __init__(self, rest):
        self.steps = rest // 2
        self.active = []
        self.waiting = []
        self.came = None
        self.started = []
        self.plan = iter(HOPS)

    def work(self, value):
        if next(self.plan):
            if self.came is not None:
                self.came = tie(*self.came, value)[:2]
            self.hop()
        started, self.started = self.started, []
        return tie(value, *started)[0] if started else value

    def pump(self, value):
        return self.hop(value) if next(self.plan) else value

    def add(self, ahead, behind, own, done):
        self.waiting.append(
            {"parts": (ahead, behind), "own": own, "rows": own.shape[0], "done": done, "hop": 0}
        )
        self.started.append(own)

    def hop(self, *values):
        if self.came is not None:
            tied = tie(*values, *self.came)
            values, self.came = tied[: len(values)], tied[len(values) :]
        rings = self.active + self.waiting
        self.waiting = []
        result = values if len(values) != 1 else values[0]
        if not rings:
            return result
        columns = rings[0]["own"].shape[1]
        moving, start, ended, plans, args = 0, 0, [], [], []
        for ring in rings:
            rows, hop = ring["rows"], ring["hop"]
            came_rows = (0, rows // 2, rows)[min(hop, 2)]
            came_at = start
            start += came_rows
            if hop == self.steps:
                plans.append((rows, came_at, came_rows, None))
                args.append(ring["own"])
                ended.append(ring)
            else:
                plans.append((rows if hop else rows // 2, came_at, came_rows, moving))
                args += [ring["parts"][side][hop] for side in range(2)]
                moving += rows if hop else rows // 2
            ring["hop"] += 1
        came = list(self.came) if self.came is not None else []
        size = sum(m.shape[0] for m in args)

        def kernel(*refs):
            came_refs = refs[: len(came)]
            part_refs = refs[len(came) : len(came) + len(args)]
            outs, local, semaphores = refs[len(came) + len(args) : -2], refs[-2], refs[-1]
            copies, at = [], 0
            for ref in part_refs:
                spot = local.at[pl.ds(at, ref.shape[0]), :]
                copies.append(pltpu.make_async_copy(ref, spot, semaphores.at[len(copies)]))
                copies[-1].start()
                at += ref.shape[0]
            wait_all(copies)
            final, at = (2 if moving else 0), 0
            for rows, came_at, came_rows, goes_to in plans:
                others = [ref[came_at : came_at + came_rows, :] for ref in came_refs] if came_rows else []
                if goes_to is None:
                    total = local[at : at + rows, :].astype(WIDE)
                    total = total + others[0].astype(WIDE) + others[1].astype(WIDE)
                    outs[final][...] = total[: rows // 2]
                    outs[final + 1][...] = total[rows // 2 :]
                    final += 2
                    at += rows
                    continue
                for side in range(2):
                    outs[side][goes_to : goes_to + rows, :] = local[at : at + rows, :]
                    if came_rows:
                        first = side * came_rows if came_rows < rows else 0
                        total = local[at + first : at + first + came_rows, :].astype(WIDE)
                        total = (total + others[side].astype(WIDE)).astype(LOW)
                        outs[side][goes_to + first : goes_to + first + came_rows, :] = total
                    at += rows

        outs = [shape_of((moving, columns), LOW)] * 2 if moving else []
        for ring in ended:
            outs += [shape_of((ring["rows"] // 2, columns), WIDE)] * 2
        scratch = [pltpu.VMEM((size, columns), LOW), pltpu.SemaphoreType.DMA((len(args),))]
        far_in = range(len(came), len(came) + len(args))
        res = call(kernel, outs, came + args, "ring_add", 0, scratch, far_in=far_in)
        at = 2 if moving else 0
        for ring in ended:
            ring["done"](res[at], res[at + 1])
            at += 2
        self.active = [ring for ring in rings if ring["hop"] <= self.steps]
        self.started += list(res[:2])
        self.came = (ring_shift(res[0], 1), ring_shift(res[1], -1)) if moving else None
        return result

    def busy(self):
        return bool(self.active or self.waiting)


def hop_places(rest):
    steps = rest // 2
    return [(1, k) for k in range(steps, 0, -1)] + [(0, k) for k in range(steps, 0, -1)] + [(0, 0)]


def rest_sum(parts):
    return lax.psum_scatter(parts, REST, scatter_dimension=0, tiled=False)


def small_gather(values):
    out = values[None]
    for axis in ("frame", "core", "inner", "outer"):
        size, here, step = lax.axis_size(axis), lax.axis_index(axis), 1
        while step < size:
            came = lax.ppermute(out, axis, [(i, i ^ step) for i in range(size)])
            first = (here & step) == 0
            out = jnp.concatenate([jnp.where(first, out, came), jnp.where(first, came, out)], axis=0)
            step *= 2
    return out


def small_sum(split, common):
    for axis in ("outer", "inner"):
        size, here = lax.axis_size(axis), lax.axis_index(axis)
        step = size // 2
        while step >= 1:
            half = split.shape[1] // 2
            bit = (here // step) % 2
            keep = lax.dynamic_slice_in_dim(split, bit * half, half, 1)
            send = lax.dynamic_slice_in_dim(split, (1 - bit) * half, half, 1)
            pairs = [(i, i ^ step) for i in range(size)]
            packed = jnp.concatenate([send.reshape(-1), common.reshape(-1)])
            came = lax.ppermute(packed, axis, pairs)
            split = keep + came[: keep.size].reshape(keep.shape)
            common = common + came[keep.size :].reshape(common.shape)
            step //= 2
    return split, common


def head_means(part, head_size):
    row = lax.broadcasted_iota(jnp.int32, (part, part), 0) // head_size
    column = lax.broadcasted_iota(jnp.int32, (part, part), 1) // head_size
    return jnp.where(row == column, 1.0 / head_size, 0.0).astype(LOW)


def head_mean(values, matrix):
    high = values.astype(LOW)
    rest = (values - high.astype(WIDE)).astype(LOW)
    return dot(high, matrix) + dot(rest, matrix)


def head_normed(values, matrix):
    center = values - head_mean(values, matrix)
    rate = lax.rsqrt(head_mean(center * center, matrix) + EPSILON)
    return center * rate, rate


def join(refs, out_ref):
    start = 0
    for ref in refs:
        out_ref[start : start + ref.shape[0], :] = ref[...]
        start += ref.shape[0]


def spans(refs):
    start = 0
    for ref in refs:
        yield start, start + ref.shape[0], ref
        start += ref.shape[0]


def flat_rows(ref, first, height, columns):
    block = ref[:, first : first + height, columns]
    return block.reshape(block.shape[0] * height, block.shape[2])


def tiles_of(total, group, block):
    for base in range(0, total, group):
        for start in range(base, base + group, block):
            yield start, base


def allowed_of(ids_col, ids_row, start, base, block, group, use_frame):
    if use_frame:
        row = lax.broadcasted_iota(jnp.int32, (block, group), 0) // FRAME_TOK
        column = lax.broadcasted_iota(jnp.int32, (block, group), 1) // FRAME_TOK
        return row == column
    return ids_col[start : start + block, :] == ids_row[:, base : base + group]


def plan(frames, rows, use_frame):
    group = min(4 * FRAME_TOK, frames * rows) if use_frame else frames * rows
    return group, min(group, 256)


def part_shapes(pieces, width):
    half = len(pieces) // 2
    return [shape_of((m.shape[0], width), WIDE if i < half else LOW) for i, m in enumerate(pieces)]


def load_semaphores(sources):
    return [pltpu.SemaphoreType.DMA((source.count,)) for source in sources]


def start_loads(sources, table_ref, far_refs, targets, semaphores):
    at, copies = 0, []
    for source, target, semaphore in zip(sources, targets, semaphores):
        copies.append(source.start(far_refs[at : at + source.count], table_ref, target, semaphore))
        at += source.count
    return copies


def attn_forward(pieces, weights, bias, head_gain, head_shift, ids, head_size, frames, use_frame, vectors=None):
    attn, proj, height, wide, table = weights
    sources = [attn] if proj is None else [attn, proj]
    far = [m for source in sources for m in source.args]
    rest, unit, _ = attn.shape
    width, part = rest * unit, head_gain.shape[-1]
    total = sum(m.shape[0] for m in pieces)
    count = len(pieces)
    group, block = plan(frames, total // (2 * frames), use_frame)
    lanes = min(128, part)
    per = lanes // head_size
    scale = head_size ** (-0.5)
    more = 0 if vectors is None else 1

    def kernel(table_ref, *refs):
        far_refs, refs = refs[: len(far)], refs[len(far) :]
        semaphores, refs = refs[-len(sources) :], refs[: -len(sources)]
        targets, refs = refs[-len(sources) :], refs[: -len(sources)]
        copies = start_loads(sources, table_ref, far_refs, targets, semaphores)
        wq, wp = targets[0], targets[-1]
        piece_refs = refs[:count]
        bias_ref, gain_ref, shift_ref, ids_col, ids_row = refs[count : count + 5]
        first, raw, qkv, lse, flat = refs[count + 5 + more : count + 10 + more]
        outs = refs[count + 10 + more :]
        if more:
            vec = refs[count + 5]
            for start, stop, ref in spans(piece_refs):
                unit_one, _ = normed(ref[...].astype(WIDE))
                value = unit_one * row_of(vec, GAIN, 0, 0) + row_of(vec, SHIFT, 0, 0)
                first[start:stop, :] = value.astype(LOW)
        else:
            join(piece_refs, first)
        matrix = head_means(part, head_size)
        for group_copies in copies:
            wait_all(group_copies)
        mixed = dot(first[...], flat_rows(wq, 0, unit, slice(0, 3 * part))) + bias_ref[...]
        raw[...] = mixed[:, : 2 * part]
        for i in range(2):
            unit_i, _ = head_normed(mixed[:, i * part : (i + 1) * part], matrix)
            value = unit_i * gain_ref[i : i + 1, :] + shift_ref[i : i + 1, :]
            qkv[:, i * part : (i + 1) * part] = value.astype(LOW)
        qkv[:, 2 * part :] = mixed[:, 2 * part :].astype(LOW)
        place = lax.broadcasted_iota(jnp.int32, (1, lanes), 1) // head_size
        for start, base in tiles_of(total, group, block):
            allowed = allowed_of(ids_col, ids_row, start, base, block, group, use_frame)
            stats = []
            for lane in range(0, part, lanes):
                query = qkv[start : start + block, lane : lane + lanes] * jnp.asarray(scale, LOW)
                key = qkv[base : base + group, part + lane : part + lane + lanes]
                value = qkv[base : base + group, 2 * part + lane : 2 * part + lane + lanes]
                out = jnp.zeros((block, lanes), WIDE)
                for h in range(per):
                    mask = place == h
                    scores = dot_nt(jnp.where(mask, query, jnp.zeros_like(query)), key)
                    scores = jnp.where(allowed, scores, -jnp.inf)
                    top = jnp.max(scores, axis=-1, keepdims=True)
                    weight = jnp.exp(scores - top)
                    norm = jnp.sum(weight, axis=-1, keepdims=True)
                    stats.append(top + jnp.log(norm))
                    probs = (weight * (1.0 / norm)).astype(LOW)
                    out = jnp.where(mask, dot(probs, value), out)
                flat[start : start + block, lane : lane + lanes] = out.astype(LOW)
            lse[start : start + block, :] = jnp.concatenate(stats, axis=1)
        for a in range(0, width, wide):
            b = a + wide
            chunk = flat_rows(wp, a // wide * height, height, slice(wp.shape[2] - wide, wp.shape[2]))
            for start, stop, ref in spans(outs):
                ref[:, a:b] = dot(flat[start:stop, :], chunk).astype(ref.dtype)

    outs = [
        shape_of((total, width), LOW),
        shape_of((total, 2 * part), WIDE),
        shape_of((total, 3 * part), LOW),
        shape_of((total, part // head_size), WIDE),
        shape_of((total, part), LOW),
    ] + part_shapes(pieces, width)
    outs += [shape_of(source.shape, LOW) for source in sources]
    args = [table] + far + list(pieces)
    args += [bias, head_gain, head_shift, ids.reshape(-1, 1), ids.reshape(1, -1)]
    args += [vectors] if more else []
    flops = 2 * total * (width * 4 * part + group * 2 * part)
    scratch = load_semaphores(sources)
    res = call(kernel, outs, args, "attn_forward", flops, scratch, 1, far_in=range(1, 1 + len(far)))
    weights = (res[5 + count], None if proj is None else res[6 + count], height, wide)
    return res[:5], res[5 : 5 + count // 2], res[5 + count // 2 : 5 + count], weights


def attn_backward(pieces, weights, head_gain, kept, ids, head_size, frames, use_frame):
    _, raw, qkv, lse, _ = kept
    attn, proj, height, wide = weights
    rest, unit, _ = attn.shape
    width, part = rest * unit, head_gain.shape[-1]
    total = sum(m.shape[0] for m in pieces)
    count = len(pieces)
    group, block = plan(frames, total // (2 * frames), use_frame)
    lanes = min(128, part)
    per = lanes // head_size
    scale = head_size ** (-0.5)
    extra = 0 if proj is None else 1

    def kernel(*refs):
        piece_refs, wq, wp = refs[:count], refs[count], refs[count + extra]
        refs = refs[extra + 1 :]
        gain_ref, raw_ref, qkv_ref, lse_ref, ids_col, ids_row = refs[count : count + 6]
        joined, low_mixed, sums, head_sums = refs[count + 6 : count + 10]
        outs = refs[count + 10 : count + 10 + count]
        grad_out, grad_three = refs[count + 10 + count :]
        join(piece_refs, joined)
        grad_flat = jnp.zeros((total, part), WIDE)
        for a in range(0, width, wide):
            b = a + wide
            chunk = flat_rows(wp, a // wide * height, height, slice(wp.shape[2] - wide, wp.shape[2]))
            grad_flat += dot_nt(joined[:, a:b], chunk)
        grad_out[...] = grad_flat.astype(LOW)
        place = lax.broadcasted_iota(jnp.int32, (1, lanes), 1) // head_size
        for start, base in tiles_of(total, group, block):
            allowed = allowed_of(ids_col, ids_row, start, base, block, group, use_frame)
            stats = lse_ref[start : start + block, :]
            for lane in range(0, part, lanes):
                query = qkv_ref[start : start + block, lane : lane + lanes] * jnp.asarray(scale, LOW)
                key = qkv_ref[base : base + group, part + lane : part + lane + lanes]
                value = qkv_ref[base : base + group, 2 * part + lane : 2 * part + lane + lanes]
                grad_here = grad_out[start : start + block, lane : lane + lanes]
                grad_q = jnp.zeros((block, lanes), WIDE)
                grad_k = jnp.zeros((group, lanes), WIDE)
                grad_v = jnp.zeros((group, lanes), WIDE)
                for h in range(per):
                    mask = place == h
                    head = lane // head_size + h
                    scores = dot_nt(jnp.where(mask, query, jnp.zeros_like(query)), key)
                    probs = jnp.exp(jnp.where(allowed, scores - stats[:, head : head + 1], -jnp.inf))
                    grad_p = dot_nt(jnp.where(mask, grad_here, jnp.zeros_like(grad_here)), value)
                    delta = jnp.sum(probs * grad_p, axis=-1, keepdims=True)
                    grad_s = (probs * (grad_p - delta)).astype(LOW)
                    grad_q = jnp.where(mask, dot(grad_s, key), grad_q)
                    grad_k = jnp.where(mask, dot_tn(grad_s, query), grad_k)
                    grad_v = jnp.where(mask, dot_tn(probs.astype(LOW), grad_here), grad_v)
                grad_three[start : start + block, lane : lane + lanes] = grad_q * scale
                for at, grad in ((part, grad_k), (2 * part, grad_v)):
                    spot = (slice(base, base + group), slice(at + lane, at + lane + lanes))
                    if start == base:
                        grad_three[spot] = grad
                    else:
                        grad_three[spot] = grad_three[spot] + grad
        matrix = head_means(part, head_size)
        for i in range(2):
            here = slice(i * part, (i + 1) * part)
            grad = grad_three[:, here]
            unit_i, rate = head_normed(raw_ref[:, here], matrix)
            head_sums[i : i + 1, :] = jnp.sum(grad * unit_i, axis=0, keepdims=True)
            head_sums[2 + i : 3 + i, :] = jnp.sum(grad, axis=0, keepdims=True)
            inner = grad * gain_ref[i : i + 1, :]
            mean_one = head_mean(inner, matrix)
            mean_two = head_mean(inner * unit_i, matrix)
            result = rate * (inner - mean_one - unit_i * mean_two)
            sums[:, here] = jnp.sum(result, axis=0, keepdims=True)
            low_mixed[:, here] = result.astype(LOW)
        result = grad_three[:, 2 * part :]
        sums[:, 2 * part :] = jnp.sum(result, axis=0, keepdims=True)
        low_mixed[:, 2 * part :] = result.astype(LOW)
        weight = flat_rows(wq, 0, unit, slice(0, 3 * part))
        for start, stop, ref in spans(outs):
            ref[...] = dot_nt(low_mixed[start:stop, :], weight).astype(ref.dtype)

    outs = [
        shape_of((total, width), LOW),
        shape_of((total, 3 * part), LOW),
        shape_of((1, 3 * part), WIDE),
        shape_of((4, part), WIDE),
    ] + part_shapes(pieces, width)
    scratch = [pltpu.VMEM((total, part), LOW), pltpu.VMEM((total, 3 * part), WIDE)]
    args = list(pieces) + [attn] + ([] if proj is None else [proj])
    args += [head_gain, raw, qkv, lse, ids.reshape(-1, 1), ids.reshape(1, -1)]
    flops = 2 * total * (width * 4 * part + group * 5 * part)
    res = call(kernel, outs, args, "attn_backward", flops, scratch)
    return res[:4], res[4 : 4 + count // 2], res[4 + count // 2 :]


def attn_weight_grads(first, low_mixed, flat, att_low, rest, height, table):
    width, part = first.shape[1], flat.shape[1]
    unit = width // rest
    wide = width * height // unit
    places = hop_places(rest)
    steps = rest // 2

    def kernel(table_ref, first_ref, mixed_ref, flat_ref, att_ref, *refs):
        outs, packed, semaphores = refs[:-2], refs[-2], refs[-1]
        product = dot_tn(first_ref[...], mixed_ref[...]).astype(LOW)
        packed[:, :, : 3 * part] = product.reshape(rest, unit, 3 * part)
        product = dot_tn(flat_ref[...], att_ref[...]).astype(LOW)
        for j in range(unit // height):
            chunk = product[:, j * wide : (j + 1) * wide].reshape(rest, height, wide)
            packed[:, j * height : (j + 1) * height, 3 * part :] = chunk
        copies = []
        for i, (side, k) in enumerate(places):
            first_row = unit // 2 if i == steps else 0
            source = packed.at[table_ref[side, k], pl.ds(first_row, outs[i].shape[0]), :]
            copies.append(pltpu.make_async_copy(source, outs[i], semaphores.at[i]))
            copies[-1].start()
        wait_all(copies)

    flops = 8 * first.shape[0] * width * part
    outs = [shape_of((unit // 2 if k == steps else unit, 4 * part), LOW) for _, k in places]
    scratch = [pltpu.VMEM((rest, unit, 4 * part), LOW), pltpu.SemaphoreType.DMA((len(places),))]
    args = [table, first, low_mixed, flat, att_low]
    res = call(kernel, outs, args, "attn_weight_grads", flops, scratch, 1, far_out=range(len(outs)))
    return res[:steps], res[steps : 2 * steps], res[2 * steps]


def mlp_weight_grads(second, pre_low, act, branch_low, rest, table):
    width, hidden = second.shape[1], act.shape[1]
    rows = width // rest
    places = hop_places(rest)
    steps = rest // 2

    def kernel(table_ref, second_ref, pre_ref, act_ref, branch_ref, *refs):
        outs, packs, semaphores = refs[:-3], refs[-3:-1], refs[-1]
        copies = []
        for which, (left, right) in enumerate(((second_ref, pre_ref), (act_ref, branch_ref))):
            pack = packs[which]
            pack[...] = dot_tn(left[...], right[...]).astype(LOW).reshape(pack.shape)
            for i, (side, k) in enumerate(places):
                if k == steps and i // steps != which:
                    continue
                spot = outs[i].at[pl.ds(0 if k == steps else which * rows, rows), :]
                source = pack.at[table_ref[side, k]]
                copies.append(pltpu.make_async_copy(source, spot, semaphores.at[len(copies)]))
                copies[-1].start()
        wait_all(copies)

    flops = 4 * second.shape[0] * width * hidden
    outs = [shape_of((rows if k == steps else 2 * rows, width), LOW) for _, k in places]
    scratch = [pltpu.VMEM((rest, rows, width), LOW)] * 2 + [pltpu.SemaphoreType.DMA((2 * len(places),))]
    args = [table, second, pre_low, act, branch_low]
    res = call(kernel, outs, args, "mlp_weight_grads", flops, scratch, 1, far_out=range(len(outs)))
    return res[:steps], res[steps : 2 * steps], res[2 * steps]


def mlp_forward(pieces, sources, table, bias):
    rest, unit, hidden = sources[0].shape
    width = rest * unit
    far = [m for source in sources for m in source.args]
    total = sum(m.shape[0] for m in pieces)
    count = len(pieces)

    def kernel(table_ref, *refs):
        far_refs, refs, (up, down), semaphores = refs[: len(far)], refs[len(far) : -4], refs[-4:-2], refs[-2:]
        copies, more_copies = start_loads(sources, table_ref, far_refs, (up, down), semaphores)
        piece_refs = refs[:count]
        bias_ref = refs[count]
        second, act, slope = refs[count + 1 : count + 4]
        outs = refs[count + 4 :]
        join(piece_refs, second)
        wait_all(copies)
        pre = dot(second[...], flat_rows(up, 0, unit, slice(None))) + bias_ref[...]
        below = 0.5 * (1.0 + lax.erf(pre * ROOT_HALF))
        act[...] = (pre * below).astype(LOW)
        slope[...] = (below + pre * (ROOT_TWO_PI * jnp.exp(-0.5 * pre * pre))).astype(LOW)
        wait_all(more_copies)
        weight = flat_rows(down, 0, down.shape[1], slice(None))
        for start, stop, ref in spans(outs):
            ref[...] = dot(act[start:stop, :], weight).astype(ref.dtype)

    outs = [
        shape_of((total, width), LOW),
        shape_of((total, hidden), LOW),
        shape_of((total, hidden), LOW),
    ] + part_shapes(pieces, width)
    outs += [shape_of(source.shape, LOW) for source in sources]
    args = [table] + far + list(pieces) + [bias]
    flops, far_in = 4 * total * width * hidden, range(1, 1 + len(far))
    res = call(kernel, outs, args, "mlp_forward", flops, load_semaphores(sources), 1, far_in=far_in)
    return res[:3], res[3 : 3 + count // 2], res[3 + count // 2 : 3 + count], res[3 + count :]


def mlp_backward(pieces, weight_up, weight_down, slope):
    rest, unit, hidden = weight_up.shape
    width = rest * unit
    total = sum(m.shape[0] for m in pieces)
    count = len(pieces)

    def kernel(*refs):
        piece_refs = refs[:count]
        up, down, slope_ref = refs[count : count + 3]
        joined, low_pre, sums = refs[count + 3 : count + 6]
        outs = refs[count + 6 :]
        join(piece_refs, joined)
        weight = flat_rows(down, 0, down.shape[1], slice(None))
        grad = dot_nt(joined[...], weight) * slope_ref[...].astype(WIDE)
        sums[...] = jnp.sum(grad, axis=0, keepdims=True)
        low_pre[...] = grad.astype(LOW)
        weight = flat_rows(up, 0, unit, slice(None))
        for start, stop, ref in spans(outs):
            ref[...] = dot_nt(low_pre[start:stop, :], weight).astype(ref.dtype)

    outs = [
        shape_of((total, width), LOW),
        shape_of((total, hidden), LOW),
        shape_of((1, hidden), WIDE),
    ] + part_shapes(pieces, width)
    args = list(pieces) + [weight_up, weight_down, slope]
    res = call(kernel, outs, args, "mlp_backward", 4 * total * width * hidden)
    return res[:3], res[3 : 3 + count // 2], res[3 + count // 2 :]


def added(refs):
    total = refs[0][...]
    for ref in refs[1:]:
        total = total + ref[...].astype(WIDE)
    return total


def row_of(vectors, kind, depth, which):
    at = kind + 2 * depth + which
    return vectors[at : at + 1, :]


def branch_norm(stream, terms, vectors, depth, which):
    after = (depth, 1) if which == 0 else (depth + 1, 0)

    def kernel(stream_ref, *refs):
        (vec, branch, result, low), term_refs = refs[-4:], refs[:-4]
        value = added(term_refs) + row_of(vec, OUT, depth, which)
        branch[...] = value
        value = stream_ref[...].astype(WIDE) + row_of(vec, SCALE, depth, which) * value
        result[...] = value
        unit, _ = normed(value)
        low[...] = (unit * row_of(vec, GAIN, *after) + row_of(vec, SHIFT, *after)).astype(LOW)

    outs = [shape_of(stream.shape, WIDE), shape_of(stream.shape, WIDE), shape_of(stream.shape, LOW)]
    return call(kernel, outs, [stream, *terms, vectors], "branch_norm")


def turn(middle, terms, cotangent, vectors):
    def kernel(middle_ref, *refs):
        (cot, vec, result, low, sums), term_refs = refs[-5:], refs[:-5]
        branch = added(term_refs) + row_of(vec, OUT, 1, 1)
        scale = row_of(vec, SCALE, 1, 1)
        result[...] = (middle_ref[...] + scale * branch).astype(LOW)
        grad = cot[...].astype(WIDE)
        grad_branch = grad * scale
        low[...] = grad_branch.astype(LOW)
        sums[0:1, :] = jnp.sum(grad * branch, axis=0, keepdims=True)
        sums[1:2, :] = jnp.sum(grad_branch, axis=0, keepdims=True)

    shape = middle.shape
    outs = [shape_of(shape, LOW), shape_of(shape, LOW), shape_of((2, shape[1]), WIDE)]
    return call(kernel, outs, [middle, *terms, cotangent, vectors], "turn")


def norm_back(grad, terms, stream, branch, vectors, depth, which, before):
    def kernel(*refs):
        grad_ref, stream_ref, vec = refs[0], refs[1], refs[2]
        inputs = 4 if before else 3
        term_refs = refs[inputs : inputs + len(terms)]
        result, low, sums = (refs[inputs + len(terms) :] + (None,))[:3] if before else (
            None, refs[inputs + len(terms)], refs[inputs + len(terms) + 1],
        )
        came = added(term_refs)
        unit, rate = normed(stream_ref[...].astype(WIDE))
        sums[0:1, :] = jnp.sum(came * unit, axis=0, keepdims=True)
        sums[1:2, :] = jnp.sum(came, axis=0, keepdims=True)
        value = grad_ref[...].astype(WIDE)
        value = value + normed_back(came, unit, rate, row_of(vec, GAIN, depth, which))
        if not before:
            low[...] = value.astype(LOW)
            return
        result[...] = value
        sums[2:3, :] = jnp.sum(value * refs[3][...], axis=0, keepdims=True)
        value = value * row_of(vec, SCALE, *before)
        sums[3:4, :] = jnp.sum(value, axis=0, keepdims=True)
        low[...] = value.astype(LOW)

    shape = grad.shape
    outs = [shape_of(shape, LOW), shape_of((4 if before else 2, shape[1]), WIDE)]
    args = [grad, stream, vectors]
    if before:
        outs = [shape_of(shape, WIDE)] + outs
        args = args + [branch]
    return call(kernel, outs, args + list(terms), "norm_back")


def split_grads(grads, me):
    rows, width = grads[0].shape[0] * len(grads) // 4, grads[0].shape[1]

    def kernel(me_ref, *refs):
        ins, outs = refs[: len(grads)], refs[len(grads) : len(grads) + 4]
        joined = refs[-1]
        join(ins, joined)
        for away, out in enumerate(outs):
            member = jnp.bitwise_xor(me_ref[0], away)
            out[...] = joined[pl.ds(pl.multiple_of(member * rows, rows), rows), :].astype(LOW)

    scratch = [pltpu.VMEM((4 * rows, width), grads[0].dtype)]
    out = shape_of((rows, width), LOW)
    return call(kernel, [out] * 4, [me, *grads], "split_grads", scratch=scratch, scalars=1)


def place_grads(qkv_pieces, up_pieces, proj, down, part, rest, me):
    rows, hidden = up_pieces[0][0].shape
    width = 4 * part
    lanes = hidden // rest

    def kernel(me_ref, *refs):
        pieces, (proj_ref, down0, down1) = refs[:16], refs[16:19]
        qkv_out, up_out, proj_out, down_out = refs[19:]
        for depth in range(2):
            for away in range(4):
                member = jnp.bitwise_xor(me_ref[0], away)
                ref = pieces[4 * depth + away]
                for s in range(3):
                    start = pl.multiple_of(s * width + member * part, 128)
                    value = ref[:, s * part : (s + 1) * part].astype(WIDE)
                    qkv_out[depth, :, pl.ds(start, part)] = value
                ref = pieces[8 + 4 * depth + away]
                for f in range(rest):
                    start = pl.multiple_of((f * 4 + member) * lanes, 128)
                    value = ref[:, f * lanes : (f + 1) * lanes].astype(WIDE)
                    up_out[depth, :, pl.ds(start, lanes)] = value
            down_out[depth] = (down0, down1)[depth][...].astype(WIDE)
        proj_out[...] = proj_ref[...].astype(WIDE)

    outs = [
        shape_of((2, rows, 3 * width), WIDE),
        shape_of((2, rows, 4 * hidden), WIDE),
        shape_of(proj.shape, WIDE),
        shape_of((2,) + down[0].shape, WIDE),
    ]
    args = [me, *qkv_pieces[0], *qkv_pieces[1], *up_pieces[0], *up_pieces[1], proj, *down]
    return call(kernel, outs, args, "place_grads", scalars=1)


def on_device(
    tokens,
    cotangent,
    scene_ids,
    frame_index,
    qkv_weight,
    qkv_bias,
    proj_weight,
    fc1_weight,
    fc1_bias,
    fc2_weight,
    out_bias,
    norm_gain,
    norm_bias,
    layer_scale,
    qk_gain,
    qk_bias,
):
    frames = lax.axis_size("frame")
    team = 2 * frames
    rest = lax.axis_size("outer") * lax.axis_size("inner")
    count = team * rest
    rows, width = tokens.shape
    head_size = qk_gain.shape[-1]
    heads = width // head_size // team
    part = heads * head_size
    hidden = fc1_weight.shape[-1] // team
    mine = lax.axis_index("core") * frames + lax.axis_index("frame")
    here = lax.axis_index("outer") * lax.axis_size("inner") + lax.axis_index("inner")
    me = mine.reshape(1).astype(jnp.int32)
    shard_rows = qkv_weight.shape[1]
    fc2_rows = fc2_weight.shape[1]
    unit = team * shard_rows
    table = ring_table()
    quick = frames == 2 and shard_rows % 32 == 0 and part % 128 == 0 and (hidden // rest) % 128 == 0
    quick = quick and hidden == width and width // count == 32 and count * rows // FRAME_TOK <= 256

    small_parts = (qkv_bias, fc1_bias, out_bias, norm_gain, norm_bias, layer_scale)
    head_gain = jnp.tile(qk_gain.astype(WIDE), (1, 1, heads))
    head_shift = jnp.tile(qk_bias.astype(WIDE), (1, 1, heads))
    weights = []
    if quick:
        proj_here = lax.ppermute(proj_weight, EVERY, spread(count, team))
        shards, below = [], None
        for depth in range(2):
            small = (qkv_bias, fc1_bias, scene_ids.reshape(1, rows)) + small_parts[2:]
            split = split_weights(depth, (qkv_weight, fc1_weight), () if depth else small, part, rest, me)
            pieces = [split[0], swap(split[1], "frame"), swap(split[2], "core"), cross(split[3])]
            if depth == 0:
                below = pieces
            shards.append(pack_weights(pieces, proj_here, fc2_weight, depth, part, me, depth == 0))
        ids = jnp.concatenate([m[shard_rows, 512 : 512 + rows] for m in below]).astype(jnp.int32)
        tokens_all = team_gather(tokens)
        rings = []
        for depth in range(2):
            attn, both = shards[depth]
            ring = RingGather(attn, unit // 2, rest)
            if depth == 0:
                steps(1, ring)
                ring.came = tie(*ring.came, *shards[1])[:2]
            came = steps(LEAD[depth] - 1 if depth == 0 else LEAD[depth], ring)
            both = tie(both, *came)[0] if came else both
            rings.append((ring, RingGather(both, unit, rest)))
            for ring in rings[depth]:
                steps(rest, ring)
        vectors, bias_qkv, bias_up = unpack_vectors(rings[0][0].rows(unit, SMALL_ROWS), table, me)
    else:
        proj_here = lax.ppermute(proj_weight, EVERY, spread(count, team))
        for depth in range(2):
            attn = exchange_columns(
                qkv_weight[depth]
                .reshape(shard_rows, 3, team, part)
                .transpose(0, 2, 1, 3)
                .reshape(shard_rows, team, 3 * part)
            ).reshape(unit, 3 * part)
            attn = jnp.concatenate([attn, widen(proj_here[depth], part)], axis=1)
            up = exchange_columns(
                fc1_weight[depth]
                .reshape(shard_rows, rest, team, hidden // rest)
                .transpose(0, 2, 1, 3)
                .reshape(shard_rows, team, hidden)
            ).reshape(unit, hidden)
            down = widen(fc2_weight[depth], hidden)
            attn, up, down = (lax.all_gather(m, REST, axis=0, tiled=False) for m in (attn, up, down))
            proj = Whole(narrow(attn[:, :, 3 * part :], shard_rows).reshape(1, part, width), 0, part)
            down = Whole(narrow(down, fc2_rows).reshape(1, hidden, width), 0, hidden)
            weights.append(((Whole(attn, 0, unit), proj, part, width, table), (Whole(up, 0, unit), down)))
        small = small_gather(jnp.concatenate([m.reshape(-1) for m in small_parts])).astype(WIDE)
        n_qkv, n_up = qkv_bias.size, fc1_bias.size
        bias_qkv = small[:, :n_qkv].reshape(count, 2, -1).transpose(1, 0, 2).reshape(2, 3, team, part)
        bias_qkv = lax.dynamic_index_in_dim(bias_qkv, mine, 2, keepdims=False).reshape(2, 3 * part)
        bias_up = small[:, n_qkv : n_qkv + n_up].reshape(rest, team, 2, -1)
        bias_up = lax.dynamic_index_in_dim(bias_up, mine, 1, keepdims=False)
        bias_up = bias_up.transpose(1, 0, 2).reshape(2, hidden)
        vectors = small[:, n_qkv + n_up :].reshape(count, 16, -1).transpose(1, 0, 2).reshape(16, width)
        ids = jnp.concatenate([m.reshape(-1) for m in team_gather(scene_ids.reshape(1, rows))])
        tokens_all = team_gather(tokens)

    gathered = []
    streams, middles, branches, kept = [tokens], [], [], []
    for depth in range(2):
        work = None
        if quick:
            attn_weights = (rings[depth][0].rows(0, unit), None, shard_rows, part, table)
        else:
            attn_weights, mlp_sources = weights[depth]
        kept_attn, own, peer, attn_weights = attn_forward(
            team_gather(low, work, work) if depth else tokens_all, attn_weights, bias_qkv[depth : depth + 1],
            head_gain[depth], head_shift[depth], ids, head_size, frames, depth == 0, None if depth else vectors,
        )
        terms = team_sum(own, peer, work)
        branch_one, middle, low = branch_norm(streams[depth], terms, vectors, depth, 0)
        pieces = team_gather(low, work, work)
        if quick:
            mlp_sources = (rings[depth][1].rows(0, unit), rings[depth][1].rows(unit, unit))
        kept_mlp, own, peer, mlp_weights = mlp_forward(pieces, mlp_sources, table, bias_up[depth : depth + 1])
        gathered.append((attn_weights, mlp_weights))
        terms = team_sum(own, peer, work)
        branch_two = None
        if depth == 0:
            branch_two, stream, low = branch_norm(middle, terms, vectors, 0, 1)
            streams.append(stream)
        middles.append(middle)
        branches.append((branch_one, branch_two))
        kept.append((kept_attn, kept_mlp))

    activations, low, turn_sums = turn(middles[1], terms, cotangent, vectors)
    grad = cotangent
    names, token_sums = [(SCALE, 1, 1), (OUT, 1, 1)], [turn_sums]
    sums_up, sums_qkv, head_sums = [None, None], [None, None], [None, None]
    finals = [{}, {}]
    ring = RingSums(rest)

    def end_mlp(depth):
        def end(up_sum, down_sum):
            if not quick:
                up = exchange_columns(up_sum.astype(LOW).reshape(team, shard_rows, hidden).transpose(1, 0, 2))
                up = up.reshape(team, shard_rows, rest, hidden // rest).transpose(1, 2, 0, 3)
                finals[depth].update(up=up.reshape(shard_rows, -1), down=narrow(down_sum, fc2_rows))
                return
            end_up(depth)(up_sum)
            finals[depth].update(down=down_sum)

        return end

    def end_up(depth):
        def end(*halves):
            m = split_grads(halves, me)
            pieces = [m[0], swap(m[1], "frame"), swap(m[2], "core"), cross(m[3])]
            ring.started += pieces[1:]
            finals[depth].update(up=pieces)

        return end

    def end_attn(depth):
        def end(low_sum, high_sum):
            if not quick:
                both = jnp.concatenate([low_sum, high_sum], axis=0)
                qkv = exchange_columns(
                    both[:, : 3 * part].astype(LOW).reshape(team, shard_rows, 3 * part).transpose(1, 0, 2)
                )
                qkv = qkv.reshape(team, shard_rows, 3, part).transpose(1, 2, 0, 3)
                proj = narrow(both[:, 3 * part :], shard_rows)
                finals[depth].update(qkv=qkv.reshape(shard_rows, -1), proj=proj.astype(LOW))
                return
            m = split_grads([low_sum[:, : 3 * part], high_sum[:, : 3 * part]], me)
            proj = jnp.concatenate([n[:, 3 * part :] for n in (low_sum, high_sum)], axis=0)
            pieces = [m[0], swap(m[1], "frame"), swap(m[2], "core"), cross(m[3])]
            ring.started += pieces[1:] if depth else []
            finals[depth].update(
                qkv=pieces,
                proj=narrow(proj, shard_rows).astype(LOW),
            )

        return end

    for depth in (1, 0):
        attn_weights, (weight_up, weight_down) = gathered[depth]
        kept_attn, (second, act, slope) = kept[depth]
        first, flat = kept_attn[0], kept_attn[4]
        pieces = team_gather(low, ring.work, ring.pump)
        (branch_low, pre_low, sum_up), own, peer = mlp_backward(pieces, weight_up, weight_down, slope)
        sums_up[depth] = sum_up
        if quick:
            mlp_parts = mlp_weight_grads(second, pre_low, act, branch_low, rest, table)
        else:
            grad_up = dot_tn(second, pre_low).astype(LOW).reshape(rest, unit, hidden)
            grad_down = dot_tn(act, branch_low).astype(LOW)
            grad_down = grad_down.reshape(rest, fc2_rows, width // hidden, hidden)
            grad_down = grad_down.transpose(0, 2, 1, 3).reshape(rest, -1, hidden)
            end_mlp(depth)(rest_sum(grad_up), rest_sum(grad_down))
        if quick:
            ring.add(*mlp_parts, end_mlp(depth))
        terms = team_sum(own, peer, ring.work, ring.pump)
        grad_middle, low, sums = norm_back(
            grad, terms, middles[depth], branches[depth][0], vectors, depth, 1, (depth, 0)
        )
        names += [(GAIN, depth, 1), (SHIFT, depth, 1), (SCALE, depth, 0), (OUT, depth, 0)]
        token_sums.append(sums)
        pieces = team_gather(low, ring.work, ring.pump)
        (att_low, mixed_low, sum_qkv, head_sum), own, peer = attn_backward(
            pieces, attn_weights, head_gain[depth], kept_attn, ids, head_size, frames, depth == 0
        )
        sums_qkv[depth], head_sums[depth] = sum_qkv, head_sum
        if quick:
            attn_parts = attn_weight_grads(first, mixed_low, flat, att_low, rest, shard_rows, table)
        else:
            grad_qkv = dot_tn(first, mixed_low).astype(LOW).reshape(rest, unit, 3 * part)
            grad_proj = dot_tn(flat, att_low).astype(LOW).reshape(rest, shard_rows, team, part)
            grad_proj = grad_proj.transpose(0, 2, 1, 3).reshape(rest, unit, part)
            attn = rest_sum(jnp.concatenate([grad_qkv, grad_proj], axis=2))
            end_attn(depth)(attn[: unit // 2], attn[unit // 2 :])
        if quick:
            ring.add(*attn_parts, end_attn(depth))
        terms = team_sum(own, peer, ring.work, ring.pump)
        if depth == 1:
            grad, low, sums = norm_back(
                grad_middle, terms, streams[1], branches[0][1], vectors, 1, 0, (0, 1)
            )
            names += [(GAIN, 1, 0), (SHIFT, 1, 0), (SCALE, 0, 1), (OUT, 0, 1)]
        else:
            input_grad, sums = norm_back(grad_middle, terms, tokens, None, vectors, 0, 0, None)
            names += [(GAIN, 0, 0), (SHIFT, 0, 0)]
        token_sums.append(sums)
    while ring.busy():
        ring.hop()

    proj_grad = lax.ppermute(
        jnp.stack([finals[0]["proj"], finals[1]["proj"]]), EVERY, [(b, a) for a, b in spread(count, team)]
    )
    if quick:
        qkv_grad, up_grad, proj_grad, down_grad = place_grads(
            [m["qkv"] for m in finals], [m["up"] for m in finals], proj_grad,
            [m["down"] for m in finals], part, rest, me,
        )
    else:
        proj_grad = proj_grad.astype(WIDE)
        qkv_grad, up_grad, down_grad = (
            jnp.stack([m[name] for m in finals]).astype(WIDE) for name in ("qkv", "up", "down")
        )

    full_qkv = lax.dynamic_update_slice(
        jnp.zeros((6, team, part), WIDE),
        jnp.concatenate(sums_qkv, axis=0).reshape(6, 1, part),
        (0, mine, 0),
    ).reshape(6, width)
    head_all = jnp.stack(head_sums).reshape(-1, heads, head_size).sum(axis=1).reshape(1, -1)
    head_all = jnp.pad(head_all, ((0, 0), (0, width - head_all.shape[1])))
    team_rows = jnp.concatenate([*token_sums, full_qkv, head_all], axis=0)
    team_rows = team_rows + swap(team_rows, "core")
    if frames == 2:
        team_rows = team_rows + swap(team_rows, "frame")
    else:
        team_rows = lax.psum(team_rows, "frame")
    sums_up = jnp.concatenate(sums_up, axis=0).reshape(2, rest, hidden // rest)
    sums_up = jnp.pad(sums_up, ((0, 0), (0, 0), (0, (width - hidden) // rest))).reshape(2, width)
    split = jnp.concatenate([team_rows[:16], sums_up], axis=0)
    split, common = small_sum(split, team_rows[16:])
    vector_grads = lax.dynamic_slice_in_dim(split[:16], mine * (width // count), width // count, 1)
    ordered = [(kind, depth, place) for kind in (OUT, GAIN, SHIFT, SCALE) for depth in (0, 1) for place in (0, 1)]
    vector_grads = jnp.stack([vector_grads[names.index(name)] for name in ordered]).reshape(4, 2, 2, -1)
    grad_bias_qkv = common[:6].reshape(2, -1)
    grad_bias_qkv = lax.dynamic_slice_in_dim(
        grad_bias_qkv, (here * team + mine) * qkv_bias.shape[1], qkv_bias.shape[1], 1
    )
    head_all = common[6, : 8 * head_size].reshape(2, 2, 2, head_size)
    return (
        activations,
        input_grad,
        qkv_grad,
        grad_bias_qkv,
        proj_grad,
        up_grad,
        split[16:, : hidden // rest],
        down_grad,
        vector_grads[0],
        vector_grads[1],
        vector_grads[2],
        vector_grads[3],
        head_all[:, 0],
        head_all[:, 1],
    )


def solution(mesh):
    scenes, frames = mesh.shape["scene"], mesh.shape["frame"]
    rest = scenes // 2
    outer = 4 if rest % 4 == 0 else rest
    grid = Mesh(mesh.devices.reshape(outer, rest // outer, 2, frames), EVERY)
    by_rows = P(EVERY, None)
    second = P(None, EVERY)
    second_rows = P(None, EVERY, None)
    last = P(None, None, EVERY)
    return jax.shard_map(
        on_device,
        mesh=grid,
        in_specs=(
            by_rows, by_rows, P(EVERY), P(EVERY), second_rows, second, second_rows, second_rows,
            second, second_rows, last, last, last, last, P(), P(),
        ),
        out_specs=(
            by_rows, by_rows, second_rows, second, second_rows, second_rows, second, second_rows,
            last, last, last, last, P(), P(),
        ),
        check_vma=False,
    )
```

profile of v0, /device:TPU:7, one launch (start us, length us, event | category | flops | bytes accessed | tf_op | source)
XLA Modules:
  0.0 426.9 jit_solution(2429908749650010927)
XLA Ops:
  6.2 5.6 %collective-permute-start.3 = (bf16[2,32,1024]{2,1,0:T(8,128)(2,1)}, bf16[2,32,1024]{2,1,0:T(8,128)(2,1)S(1)}, u32[]{:S(2)}, u32[]{:S(2)}) collective-permute-start(bf16[2,32,1024]{2,1,0:T(8,128)(2,1)} %param.22), channel_id=1, source_target_pairs={{0,0},{1,4},{2,8},{3,12},{4,16},{5,20},{6,24},{7,28},{8,1},{9,5},{... | collective-permute-start | bytes 393224 | tf_op jit(solution)/shard_map/ppermute | solution.py:1051
  11.8 4.6 %collective-permute-done.3.proj_ref = bf16[2,32,1024]{2,1,0:T(8,128)(2,1)S(1)} collective-permute-done((bf16[2,32,1024]{2,1,0:T(8,128)(2,1)}, bf16[2,32,1024]{2,1,0:T(8,128)(2,1)S(1)}, u32[]{:S(2)}, u32[]{:S(2)}) %collective-permute-start.3) | collective-permute-done | bytes 131104 | tf_op jit(solution)/shard_map/ppermute | solution.py:1051
  23.7 2.4 collective-permute-done.4.refs_1_
  37.8 4.5 %collective-permute-done.11.refs_3_ = bf16[144,1024]{1,0:T(8,128)(2,1)S(1)} collective-permute-done((bf16[144,1024]{1,0:T(8,128)(2,1)}, bf16[144,1024]{1,0:T(8,128)(2,1)S(1)}, u32[]{:S(2)}, u32[]{:S(2)}) %collective-permute-start.11) | collective-permute-done | bytes 294944 | tf_op jit(solution)/shard_map/ppermute | solution.py:272
  44.2 3.2 collective-permute-done.13.refs_7_
  49.0 6.8 %collective-permute-start.17 = (bf16[128,1024]{1,0:T(8,128)(2,1)}, bf16[128,1024]{1,0:T(8,128)(2,1)S(1)}, u32[]{:S(2)}, u32[]{:S(2)}) collective-permute-start(bf16[128,1024]{1,0:T(8,128)(2,1)} %collective-permute-done.15.refs_10_), channel_id=1, source_target_pairs={{0,2},{2,0},{1,3},{3,1},{4,6},{6,4},{5,7},{7,5},{8,10},{10,8},{9,1... | collective-permute-start | bytes 786440 | tf_op jit(solution)/shard_map/ppermute | solution.py:79
  60.8 6.8 %attn_forward.2 = (bf16[512,1024]{1,0:T(8,128)(2,1)S(1)}, f32[512,512]{1,0:T(8,128)S(1)}, bf16[512,768]{1,0:T(8,128)(2,1)S(1)}, f32[512,4]{1,0:T(8,128)S(1)}, bf...) custom-call(s32[2,8]{1,0:T(2,128)S(1)} %fusion.1.table_ref, ...), custom_call_target="tpu_custom_call" | custom-call | flops 1207959552 | bytes 10308672 | tf_op jit(solution)/shard_map/attn_forward/pallas_call | solution.py:66
  69.1 8.5 %collective-permute-start.19 = (bf16[128,1024]{1,0:T(8,128)(2,1)S(1)}, bf16[128,1024]{1,0:T(8,128)(2,1)S(1)}, u32[]{:S(2)}, u32[]{:S(2)}) collective-permute-start(bf16[128,1024]{1,0:T(8,128)(2,1)S(1)} %get-tuple-element.304), channel_id=1, source_target_pairs={{0,2},{2,0},{1,3},{3,1},{4,6},{6,4},{5,7},{7,5},{8,10},{10,8},{9,1... | collective-permute-start | bytes 786440 | tf_op jit(solution)/shard_map/ppermute | solution.py:79
  81.5 3.9 collective-permute-done.35.refs_1_
  88.1 3.8 collective-permute-done.20.refs_2_
  94.3 2.4 collective-permute-done.25.refs_3_.refs_11_
  99.7 2.6 collective-permute-done.37.refs_2_
  110.0 6.0 %mlp_forward.2 = (bf16[512,1024]{1,0:T(8,128)(2,1)S(1)}, bf16[512,1024]{1,0:T(8,128)(2,1)S(1)}, bf16[512,1024]{1,0:T(8,128)(2,1)S(1)}, f32[128,1024]{1,0:T(8,128...) custom-call(s32[2,8]{1,0:T(2,128)S(1)} %fusion.1.table_ref, ...), custom_call_target="tpu_custom_call" | custom-call | flops 2147483648 | bytes 17829952 | tf_op jit(solution)/shard_map/mlp_forward/pallas_call | solution.py:66
  128.3 3.0 collective-permute-done.34.refs_2_
  135.7 5.7 %collective-permute-done.43.refs_10_ = bf16[128,1024]{1,0:T(8,128)(2,1)} collective-permute-done((bf16[128,1024]{1,0:T(8,128)(2,1)}, bf16[128,1024]{1,0:T(8,128)(2,1)}, u32[]{:S(2)}, u32[]{:S(2)}) %collective-permute-start.43) | collective-permute-done | bytes 262176 | tf_op jit(solution)/shard_map/ppermute | solution.py:79
  144.7 6.2 %attn_forward.3 = (bf16[512,1024]{1,0:T(8,128)(2,1)S(1)}, f32[512,512]{1,0:T(8,128)S(1)}, bf16[512,768]{1,0:T(8,128)(2,1)S(1)}, f32[512,4]{1,0:T(8,128)S(1)}, bf...) custom-call(s32[2,8]{1,0:T(2,128)S(1)} %fusion.1.table_ref, ...), custom_call_target="tpu_custom_call" | custom-call | flops 1207959552 | bytes 9980992 | tf_op jit(solution)/shard_map/attn_forward/pallas_call | solution.py:66
  151.6 5.2 %collective-permute-done.51.refs_2_.refs_10_ = bf16[256,1024]{1,0:T(8,128)(2,1)} collective-permute-done((bf16[256,1024]{1,0:T(8,128)(2,1)}, bf16[256,1024]{1,0:T(8,128)(2,1)}, u32[]{:S(2)}, u32[]{:S(2)}) %collective-permute-start.51) | collective-permute-done | bytes 524320 | tf_op jit(solution)/shard_map/ppermute | solution.py:272
  161.7 6.9 %collective-permute-done.48.refs_2_ = bf16[128,1024]{1,0:T(8,128)(2,1)S(1)} collective-permute-done((bf16[128,1024]{1,0:T(8,128)(2,1)S(1)}, bf16[128,1024]{1,0:T(8,128)(2,1)S(1)}, u32[]{:S(2)}, u32[]{:S(2)}) %collective-permute-start.48) | collective-permute-done | bytes 262176 | tf_op jit(solution)/shard_map/ppermute | solution.py:79
  172.7 2.9 collective-permute-start.58
  178.9 6.1 %mlp_forward.3 = (bf16[512,1024]{1,0:T(8,128)(2,1)S(1)}, bf16[512,1024]{1,0:T(8,128)(2,1)S(1)}, bf16[512,1024]{1,0:T(8,128)(2,1)S(1)}, f32[128,1024]{1,0:T(8,128...) custom-call(s32[2,8]{1,0:T(2,128)S(1)} %fusion.1.table_ref, ...), custom_call_target="tpu_custom_call" | custom-call | flops 2147483648 | bytes 17829952 | tf_op jit(solution)/shard_map/mlp_forward/pallas_call | solution.py:66
  185.0 3.4 collective-permute-start.61
  189.9 7.3 %collective-permute-done.62.refs_2_ = bf16[128,1024]{1,0:T(8,128)(2,1)S(1)} collective-permute-done((bf16[128,1024]{1,0:T(8,128)(2,1)S(1)}, bf16[128,1024]{1,0:T(8,128)(2,1)S(1)}, u32[]{:S(2)}, u32[]{:S(2)}) %collective-permute-start.62) | collective-permute-done | bytes 262176 | tf_op jit(solution)/shard_map/ppermute | solution.py:79
  199.7 4.9 %collective-permute-done.63.refs_1_ = bf16[128,1024]{1,0:T(8,128)(2,1)S(1)} collective-permute-done((bf16[128,1024]{1,0:T(8,128)(2,1)S(1)}, bf16[128,1024]{1,0:T(8,128)(2,1)S(1)}, u32[]{:S(2)}, u32[]{:S(2)}) %collective-permute-start.63) | collective-permute-done | bytes 262176 | tf_op jit(solution)/shard_map/ppermute | solution.py:79
  207.9 4.0 mlp_backward.2
  212.3 4.6 %mlp_weight_grads.2 = (bf16[128,1024]{1,0:T(8,128)(2,1)}, bf16[256,1024]{1,0:T(8,128)(2,1)}, bf16[256,1024]{1,0:T(8,128)(2,1)}, bf16[256,1024]{1,0:T(8,128)(2,1)...) custom-call(s32[2,8]{1,0:T(2,128)S(1)} %fusion.1.table_ref, ...), custom_call_target="tpu_custom_call" | custom-call | flops 2147483648 | bytes 8388672 | tf_op jit(solution)/shard_map/mlp_weight_grads/pallas_call | solution.py:66
  220.0 5.9 %collective-permute-done.68.refs_6_ = bf16[128,1024]{1,0:T(8,128)(2,1)S(1)} collective-permute-done((bf16[128,1024]{1,0:T(8,128)(2,1)S(1)}, bf16[128,1024]{1,0:T(8,128)(2,1)S(1)}, u32[]{:S(2)}, u32[]{:S(2)}) %collective-permute-start.68) | collective-permute-done | bytes 262176 | tf_op jit(solution)/shard_map/ppermute | solution.py:79
  229.7 3.5 collective-permute-done.69.refs_1_
  236.9 7.5 %attn_backward.2 = (bf16[512,1024]{1,0:T(8,128)(2,1)S(1)}, bf16[512,768]{1,0:T(8,128)(2,1)S(1)}, f32[1,768]{1,0:T(1,128)S(1)}, f32[4,256]{1,0:T(4,128)S(1)}, f32...) custom-call(bf16[128,1024]{1,0:T(8,128)(2,1)S(1)} %get-tuple-element, ...), custom_call_target="tpu_custom_call" | custom-call | flops 1409286144 | bytes 8410112 | tf_op jit(solution)/shard_map/attn_backward/pallas_call | solution.py:66
  245.1 3.8 collective-permute-done.74.refs_0_
  249.0 3.3 attn_weight_grads.2
  258.3 6.9 %collective-permute-done.78.refs_6_ = bf16[128,1024]{1,0:T(8,128)(2,1)S(1)} collective-permute-done((bf16[128,1024]{1,0:T(8,128)(2,1)S(1)}, bf16[128,1024]{1,0:T(8,128)(2,1)S(1)}, u32[]{:S(2)}, u32[]{:S(2)}) %collective-permute-start.78) | collective-permute-done | bytes 262176 | tf_op jit(solution)/shard_map/ppermute | solution.py:79
  266.3 2.9 collective-permute-done.80.refs_0_
  272.6 2.9 collective-permute-start.82
  277.1 3.9 mlp_backward.3
  281.5 4.6 %mlp_weight_grads.3 = (bf16[128,1024]{1,0:T(8,128)(2,1)}, bf16[256,1024]{1,0:T(8,128)(2,1)}, bf16[256,1024]{1,0:T(8,128)(2,1)}, bf16[256,1024]{1,0:T(8,128)(2,1)...) custom-call(s32[2,8]{1,0:T(2,128)S(1)} %fusion.1.table_ref, ...), custom_call_target="tpu_custom_call" | custom-call | flops 2147483648 | bytes 8388672 | tf_op jit(solution)/shard_map/mlp_weight_grads/pallas_call | solution.py:66
  293.3 4.4 %collective-permute-start.87 = (bf16[32,1024]{1,0:T(8,128)(2,1)S(1)}, bf16[32,1024]{1,0:T(8,128)(2,1)S(1)}, u32[]{:S(2)}, u32[]{:S(2)}) collective-permute-start(bf16[32,1024]{1,0:T(8,128)(2,1)S(1)} %get-tuple-element.441), channel_id=1, source_target_pairs={{0,2},{2,0},{1,3},{3,1},{4,6},{6,4},{5,7},{7,5},{8,10},{10,8},{9,1... | collective-permute-start | bytes 196616 | tf_op jit(solution)/shard_map/ppermute | solution.py:79
  299.1 3.1 collective-permute-done.88.refs_15_
  302.6 2.6 collective-permute-done.91.refs_6_
  310.3 4.1 collective-permute-start.95
  316.7 7.8 %attn_backward.3 = (bf16[512,1024]{1,0:T(8,128)(2,1)S(1)}, bf16[512,768]{1,0:T(8,128)(2,1)S(1)}, f32[1,768]{1,0:T(1,128)S(1)}, f32[4,256]{1,0:T(4,128)S(1)}, f32...) custom-call(bf16[128,1024]{1,0:T(8,128)(2,1)S(1)} %get-tuple-element., ...), custom_call_target="tpu_custom_call" | custom-call | flops 1409286144 | bytes 8410112 | tf_op jit(solution)/shard_map/attn_backward/pallas_call | solution.py:66
  326.1 3.2 attn_weight_grads.3
  338.8 3.7 collective-permute-done.104.refs_5_
  350.9 13.9 %collective-permute-done.122 = f32[16384]{0:T(1024)S(1)} collective-permute-done((f32[16384]{0:T(1024)S(1)}, f32[16384]{0:T(1024)S(1)}, u32[]{:S(2)}, u32[]{:S(2)}) %collective-permute-start.122) | collective-permute-done | bytes 65568 | tf_op jit(solution)/shard_map/ppermute | solution.py:497
  364.9 2.4 ring_add.18
  368.9 15.8 %collective-permute-done.123 = f32[11776]{0:T(1024)S(1)} collective-permute-done((f32[11776]{0:T(1024)S(1)}, f32[11776]{0:T(1024)S(1)}, u32[]{:S(2)}, u32[]{:S(2)}) %collective-permute-start.123) | collective-permute-done | bytes 47136 | tf_op jit(solution)/shard_map/ppermute | solution.py:497
  400.2 7.1 %collective-permute-start.117 = (bf16[32,1024]{1,0:T(8,128)(2,1)S(1)}, bf16[32,1024]{1,0:T(8,128)(2,1)S(1)}, u32[]{:S(2)}, u32[]{:S(2)}) collective-permute-start(bf16[32,1024]{1,0:T(8,128)(2,1)S(1)} %get-tuple-element.522), channel_id=1, source_target_pairs={{0,2},{2,0},{1,3},{3,1},{4,6},{6,4},{5,7},{7,5},{8,10},{10,8},{9,1... | collective-permute-start | bytes 196616 | tf_op jit(solution)/shard_map/ppermute | solution.py:79
  409.4 4.3 %collective-permute-start.119 = (bf16[2,32,1024]{2,1,0:T(8,128)(2,1)S(1)}, bf16[2,32,1024]{2,1,0:T(8,128)(2,1)S(1)}, u32[]{:S(2)}, u32[]{:S(2)}) collective-permute-start(bf16[2,32,1024]{2,1,0:T(8,128)(2,1)S(1)} %pad_maximum_fusion), channel_id=1, source_target_pairs={{0,0},{4,1},{8,2},{12,3},{16,4},{20,5},{24,6},{28,7},{1,8},{5,9},{... | collective-permute-start | bytes 393224 | tf_op jit(solution)/shard_map/ppermute | solution.py:1236
  420.3 3.3 collective-permute-done.118.refs_11_
  (554 shorter events, 182.2 us)
Async XLA Ops:
  3.8 12.6 %collective-permute-start = (bf16[48,1792]{1,0:T(8,128)(2,1)S(1)}, bf16[48,1792]{1,0:T(8,128)(2,1)S(1)}, u32[]{:S(2)}, u32[]{:S(2)}) collective-permute-start(bf16[48,1792]{1,0:T(8,128)(2,1)S(1)} %get-tuple-element.279), channel_id=1, source_target_pairs={{0,1},{1,0},{2,3},{3,2},{4,5},{5,4},{6,7},{7,6},{8,9},{9,8},{10,11... | collective-permute-start | bytes 516104 | tf_op jit(solution)/shard_map/ppermute | solution.py:79
  4.1 12.3 %collective-permute-start.1 = (bf16[48,1792]{1,0:T(8,128)(2,1)S(1)}, bf16[48,1792]{1,0:T(8,128)(2,1)S(1)}, u32[]{:S(2)}, u32[]{:S(2)}) collective-permute-start(bf16[48,1792]{1,0:T(8,128)(2,1)S(1)} %get-tuple-element.280), channel_id=1, source_target_pairs={{0,2},{2,0},{1,3},{3,1},{4,6},{6,4},{5,7},{7,5},{8,10},{10,8},{9,1... | collective-permute-start | bytes 516104 | tf_op jit(solution)/shard_map/ppermute | solution.py:79
  5.1 11.3 %collective-permute-start.2 = (bf16[48,1792]{1,0:T(8,128)(2,1)S(1)}, bf16[48,1792]{1,0:T(8,128)(2,1)S(1)}, u32[]{:S(2)}, u32[]{:S(2)}) collective-permute-start(bf16[48,1792]{1,0:T(8,128)(2,1)S(1)} %get-tuple-element.281), channel_id=1, source_target_pairs={{0,3},{1,2},{2,1},{3,0},{4,7},{5,6},{6,5},{7,4},{8,11},{9,10},{10,... | collective-permute-start | bytes 516104 | tf_op jit(solution)/shard_map/ppermute | solution.py:83
  6.2 10.2 %collective-permute-start.3 = (bf16[2,32,1024]{2,1,0:T(8,128)(2,1)}, bf16[2,32,1024]{2,1,0:T(8,128)(2,1)S(1)}, u32[]{:S(2)}, u32[]{:S(2)}) collective-permute-start(bf16[2,32,1024]{2,1,0:T(8,128)(2,1)} %param.22), channel_id=1, source_target_pairs={{0,0},{1,4},{2,8},{3,12},{4,16},{5,20},{6,24},{7,28},{8,1},{9,5},{... | collective-permute-start | bytes 393224 | tf_op jit(solution)/shard_map/ppermute | solution.py:1051
  29.0 20.0 %collective-permute-start.15 = (bf16[128,1024]{1,0:T(8,128)(2,1)S(1)}, bf16[128,1024]{1,0:T(8,128)(2,1)}, u32[]{:S(2)}, u32[]{:S(2)}) collective-permute-start(bf16[128,1024]{1,0:T(8,128)(2,1)S(1)} %copy-done.13), channel_id=1, source_target_pairs={{0,1},{1,0},{2,3},{3,2},{4,5},{5,4},{6,7},{7,6},{8,9},{9,8},{10,11... | collective-permute-start | bytes 786440 | tf_op jit(solution)/shard_map/ppermute | solution.py:79
  30.7 28.4 %collective-permute-start.16 = (bf16[128,1024]{1,0:T(8,128)(2,1)S(1)}, bf16[128,1024]{1,0:T(8,128)(2,1)}, u32[]{:S(2)}, u32[]{:S(2)}) collective-permute-start(bf16[128,1024]{1,0:T(8,128)(2,1)S(1)} %copy-done.13), channel_id=1, source_target_pairs={{0,2},{2,0},{1,3},{3,1},{4,6},{6,4},{5,7},{7,5},{8,10},{10,8},{9,1... | collective-permute-start | bytes 786440 | tf_op jit(solution)/shard_map/ppermute | solution.py:79
  47.4 10.2 %collective-permute-start.21 = (bf16[256,1024]{1,0:T(8,128)(2,1)S(1)}, bf16[256,1024]{1,0:T(8,128)(2,1)}, u32[]{:S(2)}, u32[]{:S(2)}) collective-permute-start(bf16[256,1024]{1,0:T(8,128)(2,1)S(1)} %get-tuple-element.307.refs_0_.refs_8_), channel_id=1, source_target_pairs={{4,12},{12,20},{20,28},{28,24},{24,16},{16,8},{8,0},{0,4},{5,13},{... | collective-permute-start | bytes 1572872 | tf_op jit(solution)/shard_map/ppermute | solution.py:272
  49.0 10.2 %collective-permute-start.17 = (bf16[128,1024]{1,0:T(8,128)(2,1)}, bf16[128,1024]{1,0:T(8,128)(2,1)S(1)}, u32[]{:S(2)}, u32[]{:S(2)}) collective-permute-start(bf16[128,1024]{1,0:T(8,128)(2,1)} %collective-permute-done.15.refs_10_), channel_id=1, source_target_pairs={{0,2},{2,0},{1,3},{3,1},{4,6},{6,4},{5,7},{7,5},{8,10},{10,8},{9,1... | collective-permute-start | bytes 786440 | tf_op jit(solution)/shard_map/ppermute | solution.py:79
  57.7 21.6 %collective-permute-start.23 = (bf16[256,1024]{1,0:T(8,128)(2,1)}, bf16[256,1024]{1,0:T(8,128)(2,1)S(1)}, u32[]{:S(2)}, u32[]{:S(2)}) collective-permute-start(bf16[256,1024]{1,0:T(8,128)(2,1)} %collective-permute-done.21.refs_1_.refs_9_), channel_id=1, source_target_pairs={{4,12},{12,20},{20,28},{28,24},{24,16},{16,8},{8,0},{0,4},{5,13},{... | collective-permute-start | bytes 1572872 | tf_op jit(solution)/shard_map/ppermute | solution.py:272
  58.4 21.3 %collective-permute-start.24 = (bf16[256,1024]{1,0:T(8,128)(2,1)}, bf16[256,1024]{1,0:T(8,128)(2,1)S(1)}, u32[]{:S(2)}, u32[]{:S(2)}) collective-permute-start(bf16[256,1024]{1,0:T(8,128)(2,1)} %collective-permute-done.22.refs_4_.refs_12_), channel_id=1, source_target_pairs={{4,0},{12,4},{20,12},{28,20},{24,28},{16,24},{8,16},{0,8},{5,1},{1... | collective-permute-start | bytes 1572872 | tf_op jit(solution)/shard_map/ppermute | solution.py:272
  69.1 12.3 %collective-permute-start.19 = (bf16[128,1024]{1,0:T(8,128)(2,1)S(1)}, bf16[128,1024]{1,0:T(8,128)(2,1)S(1)}, u32[]{:S(2)}, u32[]{:S(2)}) collective-permute-start(bf16[128,1024]{1,0:T(8,128)(2,1)S(1)} %get-tuple-element.304), channel_id=1, source_target_pairs={{0,2},{2,0},{1,3},{3,1},{4,6},{6,4},{5,7},{7,5},{8,10},{10,8},{9,1... | collective-permute-start | bytes 786440 | tf_op jit(solution)/shard_map/ppermute | solution.py:79
  79.7 16.9 %collective-permute-start.25 = (bf16[256,1024]{1,0:T(8,128)(2,1)S(1)}, bf16[256,1024]{1,0:T(8,128)(2,1)S(1)}, u32[]{:S(2)}, u32[]{:S(2)}) collective-permute-start(bf16[256,1024]{1,0:T(8,128)(2,1)S(1)} %collective-permute-done.23.refs_2_.refs_10_), channel_id=1, source_target_pairs={{4,12},{12,20},{20,28},{28,24},{24,16},{16,8},{8,0},{0,4},{5,13},{... | collective-permute-start | bytes 1572872 | tf_op jit(solution)/shard_map/ppermute | solution.py:272
  81.4 16.7 %collective-permute-start.26 = (bf16[256,1024]{1,0:T(8,128)(2,1)S(1)}, bf16[256,1024]{1,0:T(8,128)(2,1)S(1)}, u32[]{:S(2)}, u32[]{:S(2)}) collective-permute-start(bf16[256,1024]{1,0:T(8,128)(2,1)S(1)} %collective-permute-done.24.refs_5_.refs_13_), channel_id=1, source_target_pairs={{4,0},{12,4},{20,12},{28,20},{24,28},{16,24},{8,16},{0,8},{5,1},{1... | collective-permute-start | bytes 1572872 | tf_op jit(solution)/shard_map/ppermute | solution.py:272
  86.8 15.4 %collective-permute-start.37 = (bf16[128,1024]{1,0:T(8,128)(2,1)S(1)}, bf16[128,1024]{1,0:T(8,128)(2,1)S(1)}, u32[]{:S(2)}, u32[]{:S(2)}) collective-permute-start(bf16[128,1024]{1,0:T(8,128)(2,1)S(1)} %collective-permute-done.35.refs_1_), channel_id=1, source_target_pairs={{4,12},{12,20},{20,28},{28,24},{24,16},{16,8},{8,0},{0,4},{5,13},{... | collective-permute-start | bytes 786440 | tf_op jit(solution)/shard_map/ppermute | solution.py:272
  92.3 11.3 %collective-permute-start.29 = (bf16[128,1024]{1,0:T(8,128)(2,1)S(1)}, bf16[128,1024]{1,0:T(8,128)(2,1)S(1)}, u32[]{:S(2)}, u32[]{:S(2)}) collective-permute-start(bf16[128,1024]{1,0:T(8,128)(2,1)S(1)} %get-tuple-element.316.refs_16_), channel_id=1, source_target_pairs={{0,1},{1,0},{2,3},{3,2},{4,5},{5,4},{6,7},{7,6},{8,9},{9,8},{10,11... | collective-permute-start | bytes 786440 | tf_op jit(solution)/shard_map/ppermute | solution.py:79
  92.9 10.8 %collective-permute-start.38 = (bf16[128,1024]{1,0:T(8,128)(2,1)S(1)}, bf16[128,1024]{1,0:T(8,128)(2,1)S(1)}, u32[]{:S(2)}, u32[]{:S(2)}) collective-permute-start(bf16[128,1024]{1,0:T(8,128)(2,1)S(1)} %collective-permute-done.36.refs_4_), channel_id=1, source_target_pairs={{4,0},{12,4},{20,12},{28,20},{24,28},{16,24},{8,16},{0,8},{5,1},{1... | collective-permute-start | bytes 786440 | tf_op jit(solution)/shard_map/ppermute | solution.py:272
  103.7 17.2 %collective-permute-start.39 = (bf16[128,1024]{1,0:T(8,128)(2,1)S(1)}, bf16[128,1024]{1,0:T(8,128)(2,1)S(1)}, u32[]{:S(2)}, u32[]{:S(2)}) collective-permute-start(bf16[128,1024]{1,0:T(8,128)(2,1)S(1)} %collective-permute-done.37.refs_2_), channel_id=1, source_target_pairs={{4,12},{12,20},{20,28},{28,24},{24,16},{16,8},{8,0},{0,4},{5,13},{... | collective-permute-start | bytes 786440 | tf_op jit(solution)/shard_map/ppermute | solution.py:272
  107.8 13.1 %collective-permute-start.40 = (bf16[128,1024]{1,0:T(8,128)(2,1)S(1)}, bf16[128,1024]{1,0:T(8,128)(2,1)S(1)}, u32[]{:S(2)}, u32[]{:S(2)}) collective-permute-start(bf16[128,1024]{1,0:T(8,128)(2,1)S(1)} %collective-permute-done.38.refs_5_), channel_id=1, source_target_pairs={{4,0},{12,4},{20,12},{28,20},{24,28},{16,24},{8,16},{0,8},{5,1},{1... | collective-permute-start | bytes 786440 | tf_op jit(solution)/shard_map/ppermute | solution.py:272
  126.8 16.2 %collective-permute-start.49 = (bf16[256,1024]{1,0:T(8,128)(2,1)S(1)}, bf16[256,1024]{1,0:T(8,128)(2,1)}, u32[]{:S(2)}, u32[]{:S(2)}) collective-permute-start(bf16[256,1024]{1,0:T(8,128)(2,1)S(1)} %get-tuple-element.337.refs_0_.refs_8_), channel_id=1, source_target_pairs={{4,12},{12,20},{20,28},{28,24},{24,16},{16,8},{8,0},{0,4},{5,13},{... | collective-permute-start | bytes 1572872 | tf_op jit(solution)/shard_map/ppermute | solution.py:272
  127.9 15.1 %collective-permute-start.50 = (bf16[256,1024]{1,0:T(8,128)(2,1)S(1)}, bf16[256,1024]{1,0:T(8,128)(2,1)}, u32[]{:S(2)}, u32[]{:S(2)}) collective-permute-start(bf16[256,1024]{1,0:T(8,128)(2,1)S(1)} %get-tuple-element.337.refs_0_.refs_8_), channel_id=1, source_target_pairs={{4,0},{12,4},{20,12},{28,20},{24,28},{16,24},{8,16},{0,8},{5,1},{1... | collective-permute-start | bytes 1572872 | tf_op jit(solution)/shard_map/ppermute | solution.py:272
  134.8 9.9 %collective-permute-start.44 = (bf16[128,1024]{1,0:T(8,128)(2,1)}, bf16[128,1024]{1,0:T(8,128)(2,1)}, u32[]{:S(2)}, u32[]{:S(2)}) collective-permute-start(bf16[128,1024]{1,0:T(8,128)(2,1)} %get-tuple-element.331.refs_9_), channel_id=1, source_target_pairs={{0,2},{2,0},{1,3},{3,1},{4,6},{6,4},{5,7},{7,5},{8,10},{10,8},{9,1... | collective-permute-start | bytes 786440 | tf_op jit(solution)/shard_map/ppermute | solution.py:79
  143.0 13.8 %collective-permute-start.51 = (bf16[256,1024]{1,0:T(8,128)(2,1)}, bf16[256,1024]{1,0:T(8,128)(2,1)}, u32[]{:S(2)}, u32[]{:S(2)}) collective-permute-start(bf16[256,1024]{1,0:T(8,128)(2,1)} %collective-permute-done.49.refs_1_.refs_9_), channel_id=1, source_target_pairs={{4,12},{12,20},{20,28},{28,24},{24,16},{16,8},{8,0},{0,4},{5,13},{... | collective-permute-start | bytes 1572872 | tf_op jit(solution)/shard_map/ppermute | solution.py:272
  143.8 13.5 %collective-permute-start.52 = (bf16[256,1024]{1,0:T(8,128)(2,1)}, bf16[256,1024]{1,0:T(8,128)(2,1)}, u32[]{:S(2)}, u32[]{:S(2)}) collective-permute-start(bf16[256,1024]{1,0:T(8,128)(2,1)} %collective-permute-done.50.refs_4_.refs_12_), channel_id=1, source_target_pairs={{4,0},{12,4},{20,12},{28,20},{24,28},{16,24},{8,16},{0,8},{5,1},{1... | collective-permute-start | bytes 1572872 | tf_op jit(solution)/shard_map/ppermute | solution.py:272
  157.3 12.5 %collective-permute-start.53 = (bf16[256,1024]{1,0:T(8,128)(2,1)}, bf16[256,1024]{1,0:T(8,128)(2,1)S(1)}, u32[]{:S(2)}, u32[]{:S(2)}) collective-permute-start(bf16[256,1024]{1,0:T(8,128)(2,1)} %collective-permute-done.51.refs_2_.refs_10_), channel_id=1, source_target_pairs={{4,12},{12,20},{20,28},{28,24},{24,16},{16,8},{8,0},{0,4},{5,13},{... | collective-permute-start | bytes 1572872 | tf_op jit(solution)/shard_map/ppermute | solution.py:272
  158.5 12.2 %collective-permute-start.54 = (bf16[256,1024]{1,0:T(8,128)(2,1)}, bf16[256,1024]{1,0:T(8,128)(2,1)S(1)}, u32[]{:S(2)}, u32[]{:S(2)}) collective-permute-start(bf16[256,1024]{1,0:T(8,128)(2,1)} %collective-permute-done.52.refs_5_.refs_13_), channel_id=1, source_target_pairs={{4,0},{12,4},{20,12},{28,20},{24,28},{16,24},{8,16},{0,8},{5,1},{1... | collective-permute-start | bytes 1572872 | tf_op jit(solution)/shard_map/ppermute | solution.py:272
  235.3 13.6 %collective-permute-start.74 = (bf16[256,1024]{1,0:T(8,128)(2,1)S(1)}, bf16[256,1024]{1,0:T(8,128)(2,1)S(1)}, u32[]{:S(2)}, u32[]{:S(2)}) collective-permute-start(bf16[256,1024]{1,0:T(8,128)(2,1)S(1)} %get-tuple-element.380), channel_id=1, source_target_pairs={{4,12},{12,20},{20,28},{28,24},{24,16},{16,8},{8,0},{0,4},{5,13},{... | collective-permute-start | bytes 1572872 | tf_op jit(solution)/shard_map/ppermute | solution.py:272
  235.6 13.4 %collective-permute-start.75 = (bf16[256,1024]{1,0:T(8,128)(2,1)S(1)}, bf16[256,1024]{1,0:T(8,128)(2,1)S(1)}, u32[]{:S(2)}, u32[]{:S(2)}) collective-permute-start(bf16[256,1024]{1,0:T(8,128)(2,1)S(1)} %get-tuple-element.381), channel_id=1, source_target_pairs={{4,0},{12,4},{20,12},{28,20},{24,28},{16,24},{8,16},{0,8},{5,1},{1... | collective-permute-start | bytes 1572872 | tf_op jit(solution)/shard_map/ppermute | solution.py:272
  244.5 12.6 %collective-permute-start.77 = (bf16[128,1024]{1,0:T(8,128)(2,1)S(1)}, bf16[128,1024]{1,0:T(8,128)(2,1)S(1)}, u32[]{:S(2)}, u32[]{:S(2)}) collective-permute-start(bf16[128,1024]{1,0:T(8,128)(2,1)S(1)} %get-tuple-element.406), channel_id=1, source_target_pairs={{0,2},{2,0},{1,3},{3,1},{4,6},{6,4},{5,7},{7,5},{8,10},{10,8},{9,1... | collective-permute-start | bytes 786440 | tf_op jit(solution)/shard_map/ppermute | solution.py:79
  253.9 15.2 %collective-permute-start.80 = (bf16[320,1024]{1,0:T(8,128)(2,1)S(1)}, bf16[320,1024]{1,0:T(8,128)(2,1)S(1)}, u32[]{:S(2)}, u32[]{:S(2)}) collective-permute-start(bf16[320,1024]{1,0:T(8,128)(2,1)S(1)} %get-tuple-element.402), channel_id=1, source_target_pairs={{4,12},{12,20},{20,28},{28,24},{24,16},{16,8},{8,0},{0,4},{5,13},{... | collective-permute-start | bytes 1966088 | tf_op jit(solution)/shard_map/ppermute | solution.py:272
  254.4 14.8 %collective-permute-start.81 = (bf16[320,1024]{1,0:T(8,128)(2,1)S(1)}, bf16[320,1024]{1,0:T(8,128)(2,1)S(1)}, u32[]{:S(2)}, u32[]{:S(2)}) collective-permute-start(bf16[320,1024]{1,0:T(8,128)(2,1)S(1)} %get-tuple-element.403), channel_id=1, source_target_pairs={{4,0},{12,4},{20,12},{28,20},{24,28},{16,24},{8,16},{0,8},{5,1},{1... | collective-permute-start | bytes 1966088 | tf_op jit(solution)/shard_map/ppermute | solution.py:272
  270.9 16.8 %collective-permute-start.84 = (bf16[384,1024]{1,0:T(8,128)(2,1)S(1)}, bf16[384,1024]{1,0:T(8,128)(2,1)S(1)}, u32[]{:S(2)}, u32[]{:S(2)}) collective-permute-start(bf16[384,1024]{1,0:T(8,128)(2,1)S(1)} %get-tuple-element.418), channel_id=1, source_target_pairs={{4,12},{12,20},{20,28},{28,24},{24,16},{16,8},{8,0},{0,4},{5,13},{... | collective-permute-start | bytes 2359304 | tf_op jit(solution)/shard_map/ppermute | solution.py:272
  271.9 16.6 %collective-permute-start.85 = (bf16[384,1024]{1,0:T(8,128)(2,1)S(1)}, bf16[384,1024]{1,0:T(8,128)(2,1)S(1)}, u32[]{:S(2)}, u32[]{:S(2)}) collective-permute-start(bf16[384,1024]{1,0:T(8,128)(2,1)S(1)} %get-tuple-element.419), channel_id=1, source_target_pairs={{4,0},{12,4},{20,12},{28,20},{24,28},{16,24},{8,16},{0,8},{5,1},{1... | collective-permute-start | bytes 2359304 | tf_op jit(solution)/shard_map/ppermute | solution.py:272
  281.1 16.6 %collective-permute-start.90 = (bf16[128,1024]{1,0:T(8,128)(2,1)S(1)}, bf16[128,1024]{1,0:T(8,128)(2,1)S(1)}, u32[]{:S(2)}, u32[]{:S(2)}) collective-permute-start(bf16[128,1024]{1,0:T(8,128)(2,1)S(1)} %get-tuple-element.447), channel_id=1, source_target_pairs={{0,2},{2,0},{1,3},{3,1},{4,6},{6,4},{5,7},{7,5},{8,10},{10,8},{9,1... | collective-permute-start | bytes 786440 | tf_op jit(solution)/shard_map/ppermute | solution.py:79
  290.3 14.8 %collective-permute-start.92 = (bf16[256,1024]{1,0:T(8,128)(2,1)S(1)}, bf16[256,1024]{1,0:T(8,128)(2,1)S(1)}, u32[]{:S(2)}, u32[]{:S(2)}) collective-permute-start(bf16[256,1024]{1,0:T(8,128)(2,1)S(1)} %get-tuple-element.443), channel_id=1, source_target_pairs={{4,12},{12,20},{20,28},{28,24},{24,16},{16,8},{8,0},{0,4},{5,13},{... | collective-permute-start | bytes 1572872 | tf_op jit(solution)/shard_map/ppermute | solution.py:272
  290.8 14.4 %collective-permute-start.93 = (bf16[256,1024]{1,0:T(8,128)(2,1)S(1)}, bf16[256,1024]{1,0:T(8,128)(2,1)S(1)}, u32[]{:S(2)}, u32[]{:S(2)}) collective-permute-start(bf16[256,1024]{1,0:T(8,128)(2,1)S(1)} %get-tuple-element.444), channel_id=1, source_target_pairs={{4,0},{12,4},{20,12},{28,20},{24,28},{16,24},{8,16},{0,8},{5,1},{1... | collective-permute-start | bytes 1572872 | tf_op jit(solution)/shard_map/ppermute | solution.py:272
  308.5 20.8 %collective-permute-start.97 = (bf16[384,1024]{1,0:T(8,128)(2,1)S(1)}, bf16[384,1024]{1,0:T(8,128)(2,1)S(1)}, u32[]{:S(2)}, u32[]{:S(2)}) collective-permute-start(bf16[384,1024]{1,0:T(8,128)(2,1)S(1)} %get-tuple-element.457), channel_id=1, source_target_pairs={{4,12},{12,20},{20,28},{28,24},{24,16},{16,8},{8,0},{0,4},{5,13},{... | collective-permute-start | bytes 2359304 | tf_op jit(solution)/shard_map/ppermute | solution.py:272
  309.0 20.4 %collective-permute-start.98 = (bf16[384,1024]{1,0:T(8,128)(2,1)S(1)}, bf16[384,1024]{1,0:T(8,128)(2,1)S(1)}, u32[]{:S(2)}, u32[]{:S(2)}) collective-permute-start(bf16[384,1024]{1,0:T(8,128)(2,1)S(1)} %get-tuple-element.458), channel_id=1, source_target_pairs={{4,0},{12,4},{20,12},{28,20},{24,28},{16,24},{8,16},{0,8},{5,1},{1... | collective-permute-start | bytes 2359304 | tf_op jit(solution)/shard_map/ppermute | solution.py:272
  347.2 17.6 %collective-permute-start.105 = (bf16[320,1024]{1,0:T(8,128)(2,1)}, bf16[320,1024]{1,0:T(8,128)(2,1)S(1)}, u32[]{:S(2)}, u32[]{:S(2)}) collective-permute-start(bf16[320,1024]{1,0:T(8,128)(2,1)} %copy-done.69), channel_id=1, source_target_pairs={{4,12},{12,20},{20,28},{28,24},{24,16},{16,8},{8,0},{0,4},{5,13},{... | collective-permute-start | bytes 1966088 | tf_op jit(solution)/shard_map/ppermute | solution.py:272
  347.7 17.2 %collective-permute-start.106 = (bf16[320,1024]{1,0:T(8,128)(2,1)S(1)}, bf16[320,1024]{1,0:T(8,128)(2,1)S(1)}, u32[]{:S(2)}, u32[]{:S(2)}) collective-permute-start(bf16[320,1024]{1,0:T(8,128)(2,1)S(1)} %get-tuple-element.485), channel_id=1, source_target_pairs={{4,0},{12,4},{20,12},{28,20},{24,28},{16,24},{8,16},{0,8},{5,1},{1... | collective-permute-start | bytes 1966088 | tf_op jit(solution)/shard_map/ppermute | solution.py:272
  350.5 14.3 %collective-permute-start.122 = (f32[16384]{0:T(1024)S(1)}, f32[16384]{0:T(1024)S(1)}, u32[]{:S(2)}, u32[]{:S(2)}) collective-permute-start(f32[16384]{0:T(1024)S(1)} %pad_maximum_fusion.4), channel_id=1, source_target_pairs={{0,16},{8,24},{16,0},{24,8},{1,17},{9,25},{17,1},{25,9},{2,18},{10... | collective-permute-start | bytes 196616 | tf_op jit(solution)/shard_map/ppermute | solution.py:497
  367.3 19.5 %collective-permute-start.107 = (bf16[384,1024]{1,0:T(8,128)(2,1)}, bf16[384,1024]{1,0:T(8,128)(2,1)S(1)}, u32[]{:S(2)}, u32[]{:S(2)}) collective-permute-start(bf16[384,1024]{1,0:T(8,128)(2,1)} %get-tuple-element.496), channel_id=1, source_target_pairs={{4,12},{12,20},{20,28},{28,24},{24,16},{16,8},{8,0},{0,4},{5,13},{... | collective-permute-start | bytes 2359304 | tf_op jit(solution)/shard_map/ppermute | solution.py:272
  367.4 19.4 %collective-permute-start.108 = (bf16[384,1024]{1,0:T(8,128)(2,1)S(1)}, bf16[384,1024]{1,0:T(8,128)(2,1)S(1)}, u32[]{:S(2)}, u32[]{:S(2)}) collective-permute-start(bf16[384,1024]{1,0:T(8,128)(2,1)S(1)} %get-tuple-element.497), channel_id=1, source_target_pairs={{4,0},{12,4},{20,12},{28,20},{24,28},{16,24},{8,16},{0,8},{5,1},{1... | collective-permute-start | bytes 2359304 | tf_op jit(solution)/shard_map/ppermute | solution.py:272
  368.8 15.9 %collective-permute-start.123 = (f32[11776]{0:T(1024)S(1)}, f32[11776]{0:T(1024)S(1)}, u32[]{:S(2)}, u32[]{:S(2)}) collective-permute-start(f32[11776]{0:T(1024)S(1)} %pad_maximum_fusion.5), channel_id=1, source_target_pairs={{0,8},{8,0},{16,24},{24,16},{1,9},{9,1},{17,25},{25,17},{2,10},{10... | collective-permute-start | bytes 141320 | tf_op jit(solution)/shard_map/ppermute | solution.py:497
  395.8 11.5 %collective-permute-start.111 = (bf16[128,1024]{1,0:T(8,128)(2,1)S(1)}, bf16[128,1024]{1,0:T(8,128)(2,1)S(1)}, u32[]{:S(2)}, u32[]{:S(2)}) collective-permute-start(bf16[128,1024]{1,0:T(8,128)(2,1)S(1)} %get-tuple-element.508), channel_id=1, source_target_pairs={{4,12},{12,20},{20,28},{28,24},{24,16},{16,8},{8,0},{0,4},{5,13},{... | collective-permute-start | bytes 786440 | tf_op jit(solution)/shard_map/ppermute | solution.py:272
  396.8 10.5 %collective-permute-start.112 = (bf16[128,1024]{1,0:T(8,128)(2,1)S(1)}, bf16[128,1024]{1,0:T(8,128)(2,1)S(1)}, u32[]{:S(2)}, u32[]{:S(2)}) collective-permute-start(bf16[128,1024]{1,0:T(8,128)(2,1)S(1)} %get-tuple-element.509), channel_id=1, source_target_pairs={{4,0},{12,4},{20,12},{28,20},{24,28},{16,24},{8,16},{0,8},{5,1},{1... | collective-permute-start | bytes 786440 | tf_op jit(solution)/shard_map/ppermute | solution.py:272
  399.3 18.0 %collective-permute-start.116 = (bf16[32,1024]{1,0:T(8,128)(2,1)}, bf16[32,1024]{1,0:T(8,128)(2,1)S(1)}, u32[]{:S(2)}, u32[]{:S(2)}) collective-permute-start(bf16[32,1024]{1,0:T(8,128)(2,1)} %get-tuple-element.521), channel_id=1, source_target_pairs={{0,1},{1,0},{2,3},{3,2},{4,5},{5,4},{6,7},{7,6},{8,9},{9,8},{10,11... | collective-permute-start | bytes 196616 | tf_op jit(solution)/shard_map/ppermute | solution.py:79
  400.2 17.9 %collective-permute-start.117 = (bf16[32,1024]{1,0:T(8,128)(2,1)S(1)}, bf16[32,1024]{1,0:T(8,128)(2,1)S(1)}, u32[]{:S(2)}, u32[]{:S(2)}) collective-permute-start(bf16[32,1024]{1,0:T(8,128)(2,1)S(1)} %get-tuple-element.522), channel_id=1, source_target_pairs={{0,2},{2,0},{1,3},{3,1},{4,6},{6,4},{5,7},{7,5},{8,10},{10,8},{9,1... | collective-permute-start | bytes 196616 | tf_op jit(solution)/shard_map/ppermute | solution.py:79
  409.4 15.0 %collective-permute-start.119 = (bf16[2,32,1024]{2,1,0:T(8,128)(2,1)S(1)}, bf16[2,32,1024]{2,1,0:T(8,128)(2,1)S(1)}, u32[]{:S(2)}, u32[]{:S(2)}) collective-permute-start(bf16[2,32,1024]{2,1,0:T(8,128)(2,1)S(1)} %pad_maximum_fusion), channel_id=1, source_target_pairs={{0,0},{4,1},{8,2},{12,3},{16,4},{20,5},{24,6},{28,7},{1,8},{5,9},{... | collective-permute-start | bytes 393224 | tf_op jit(solution)/shard_map/ppermute | solution.py:1236
  (179 other events, 1953.0 us)
where the time goes:
time: 434 us; the launch traced here: 427 us
  waiting for transfers between devices  156 us (36%)
  starting transfers between devices  146 us (34%)
  Pallas kernels  92.5 us (21%)
  local copies, waits for them, and re-layouts  25.3 us (6%)
  other arithmetic  4.73 us (1%)
    pallas_call x41, Pallas kernels, call(): pl.pallas_call(kernel, out_shape=list(outs), in_specs=in_specs, out_specs...  92.5 us
    ppermute x62, starting transfers between devices, swap(): return lax.ppermute(values, axis, [(0, 1), (1, 0)])  84.4 us
    ppermute x62, waiting for transfers between devices, swap(): return lax.ppermute(values, axis, [(0, 1), (1, 0)])  64.6 us
    ppermute x52, waiting for transfers between devices, ring_shift(): lax.ppermute(values, REST, [(order[i], order[(i + sign) % rest]) for i in...  49.8 us
    ppermute x52, starting transfers between devices, ring_shift(): lax.ppermute(values, REST, [(order[i], order[(i + sign) % rest]) for i in...  43.6 us
    ppermute x3, waiting for transfers between devices, small_sum(): came = lax.ppermute(packed, axis, pairs)  29.6 us
    unnamed x205, local copies, waits for them, and re-layouts  18.5 us
  transfers between devices with their start and end apart: 125, of which 58 were waited for; matrix products, arithmetic and copies ran while one was open for 3% of the time, Pallas kernels for 17%

commit v1 on v0

--- a/solution.py
+++ b/solution.py
@@ -978,8 +978,8 @@
     lanes = hidden // rest
 
     def kernel(me_ref, *refs):
-        pieces, (proj_ref, down0, down1) = refs[:16], refs[16:19]
-        qkv_out, up_out, proj_out, down_out = refs[19:]
+        pieces, (proj0, proj1, down0, down1) = refs[:16], refs[16:20]
+        qkv_out, up_out, proj_out, down_out = refs[20:]
         for depth in range(2):
             for away in range(4):
                 member = jnp.bitwise_xor(me_ref[0], away)
@@ -994,15 +994,15 @@
                     value = ref[:, f * lanes : (f + 1) * lanes].astype(WIDE)
                     up_out[depth, :, pl.ds(start, lanes)] = value
             down_out[depth] = (down0, down1)[depth][...].astype(WIDE)
-        proj_out[...] = proj_ref[...].astype(WIDE)
+            proj_out[depth] = (proj0, proj1)[depth][...].astype(WIDE)
 
     outs = [
         shape_of((2, rows, 3 * width), WIDE),
         shape_of((2, rows, 4 * hidden), WIDE),
-        shape_of(proj.shape, WIDE),
+        shape_of((2,) + proj[0].shape, WIDE),
         shape_of((2,) + down[0].shape, WIDE),
     ]
-    args = [me, *qkv_pieces[0], *qkv_pieces[1], *up_pieces[0], *up_pieces[1], proj, *down]
+    args = [me, *qkv_pieces[0], *qkv_pieces[1], *up_pieces[0], *up_pieces[1], *proj, *down]
     return call(kernel, outs, args, "place_grads", scalars=1)
 
 
@@ -1139,6 +1139,8 @@
     finals = [{}, {}]
     ring = RingSums(rest)
 
+    home = [(b, a) for a, b in spread(count, team)]
+
     def end_mlp(depth):
         def end(up_sum, down_sum):
             if not quick:
@@ -1169,7 +1171,8 @@
                 )
                 qkv = qkv.reshape(team, shard_rows, 3, part).transpose(1, 2, 0, 3)
                 proj = narrow(both[:, 3 * part :], shard_rows)
-                finals[depth].update(qkv=qkv.reshape(shard_rows, -1), proj=proj.astype(LOW))
+                proj = lax.ppermute(proj.astype(LOW), EVERY, home)
+                finals[depth].update(qkv=qkv.reshape(shard_rows, -1), proj=proj)
                 return
             m = split_grads([low_sum[:, : 3 * part], high_sum[:, : 3 * part]], me)
             proj = jnp.concatenate([n[:, 3 * part :] for n in (low_sum, high_sum)], axis=0)
@@ -1177,7 +1180,7 @@
             ring.started += pieces[1:] if depth else []
             finals[depth].update(
                 qkv=pieces,
-                proj=narrow(proj, shard_rows).astype(LOW),
+                proj=lax.ppermute(narrow(proj, shard_rows).astype(LOW), EVERY, home),
             )
 
         return end
@@ -1233,16 +1236,13 @@
     while ring.busy():
         ring.hop()
 
-    proj_grad = lax.ppermute(
-        jnp.stack([finals[0]["proj"], finals[1]["proj"]]), EVERY, [(b, a) for a, b in spread(count, team)]
-    )
     if quick:
         qkv_grad, up_grad, proj_grad, down_grad = place_grads(
-            [m["qkv"] for m in finals], [m["up"] for m in finals], proj_grad,
+            [m["qkv"] for m in finals], [m["up"] for m in finals], [m["proj"] for m in finals],
             [m["down"] for m in finals], part, rest, me,
         )
     else:
-        proj_grad = proj_grad.astype(WIDE)
+        proj_grad = jnp.stack([m["proj"] for m in finals]).astype(WIDE)
         qkv_grad, up_grad, down_grad = (
             jnp.stack([m[name] for m in finals]).astype(WIDE) for name in ("qkv", "up", "down")
         )

time: 434 us -> 434 us (level)
  starting transfers between devices: 146 us -> 151 us
    ppermute x1 -> x2, starting transfers between devices: 4.3 us -> 10.7 us  [end(): lax.ppermute(narrow(proj, shard_rows).astype(LOW), EVERY, home)]
    unnamed x205 -> x211, local copies, waits for them, and re-layouts: 18.5 us -> 20.3 us
  transfers between devices with their start and end apart: 125 -> 126, of which waited for: 58 -> 61; matrix products, arithmetic and copies ran while one was open for 3% -> 2% of each run, Pallas kernels for 17% -> 17%
where the time goes in v1:
time: 434 us; the launch traced here: 426 us
  waiting for transfers between devices  152 us (35%)
  starting transfers between devices  151 us (35%)
  Pallas kernels  91.8 us (21%)
  local copies, waits for them, and re-layouts  26.5 us (6%)
    pallas_call x41, Pallas kernels, call(): pl.pallas_call(kernel, out_shape=list(outs), in_specs=in_specs, out_specs...  91.8 us
    ppermute x62, starting transfers between devices, swap(): return lax.ppermute(values, axis, [(0, 1), (1, 0)])  83.2 us
    ppermute x62, waiting for transfers between devices, swap(): return lax.ppermute(values, axis, [(0, 1), (1, 0)])  66.6 us
    ppermute x52, waiting for transfers between devices, ring_shift(): lax.ppermute(values, REST, [(order[i], order[(i + sign) % rest]) for i in...  51.1 us
    ppermute x52, starting transfers between devices, ring_shift(): lax.ppermute(values, REST, [(order[i], order[(i + sign) % rest]) for i in...  44 us
    ppermute x3, waiting for transfers between devices, small_sum(): came = lax.ppermute(packed, axis, pairs)  25.4 us
    unnamed x211, local copies, waits for them, and re-layouts  20.3 us
    ppermute x2, starting transfers between devices, end(): lax.ppermute(narrow(proj, shard_rows).astype(LOW), EVERY, home)  10.7 us
  transfers between devices with their start and end apart: 126, of which 61 were waited for; matrix products, arithmetic and copies ran while one was open for 2% of the time, Pallas kernels for 17%

profile of v1, /device:TPU:7, one launch (start us, length us, event | category | flops | bytes accessed | tf_op | source)
XLA Modules:
  0.0 426.4 jit_solution(733449382992909363)
XLA Ops:
  6.2 5.6 %collective-permute-start.3 = (bf16[2,32,1024]{2,1,0:T(8,128)(2,1)}, bf16[2,32,1024]{2,1,0:T(8,128)(2,1)S(1)}, u32[]{:S(2)}, u32[]{:S(2)}) collective-permute-start(bf16[2,32,1024]{2,1,0:T(8,128)(2,1)} %param.22), channel_id=1, source_target_pairs={{0,0},{1,4},{2,8},{3,12},{4,16},{5,20},{6,24},{7,28},{8,1},{9,5},{... | collective-permute-start | bytes 393224 | tf_op jit(solution)/shard_map/ppermute | solution.py:1051
  11.8 4.6 %collective-permute-done.3.proj_ref = bf16[2,32,1024]{2,1,0:T(8,128)(2,1)S(1)} collective-permute-done((bf16[2,32,1024]{2,1,0:T(8,128)(2,1)}, bf16[2,32,1024]{2,1,0:T(8,128)(2,1)S(1)}, u32[]{:S(2)}, u32[]{:S(2)}) %collective-permute-start.3) | collective-permute-done | bytes 131104 | tf_op jit(solution)/shard_map/ppermute | solution.py:1051
  37.8 4.5 %collective-permute-done.11.refs_3_ = bf16[144,1024]{1,0:T(8,128)(2,1)S(1)} collective-permute-done((bf16[144,1024]{1,0:T(8,128)(2,1)}, bf16[144,1024]{1,0:T(8,128)(2,1)S(1)}, u32[]{:S(2)}, u32[]{:S(2)}) %collective-permute-start.11) | collective-permute-done | bytes 294944 | tf_op jit(solution)/shard_map/ppermute | solution.py:272
  44.2 3.2 collective-permute-done.13.refs_7_
  49.0 6.8 %collective-permute-start.17 = (bf16[128,1024]{1,0:T(8,128)(2,1)}, bf16[128,1024]{1,0:T(8,128)(2,1)S(1)}, u32[]{:S(2)}, u32[]{:S(2)}) collective-permute-start(bf16[128,1024]{1,0:T(8,128)(2,1)} %collective-permute-done.15.refs_10_), channel_id=1, source_target_pairs={{0,2},{2,0},{1,3},{3,1},{4,6},{6,4},{5,7},{7,5},{8,10},{10,8},{9,1... | collective-permute-start | bytes 786440 | tf_op jit(solution)/shard_map/ppermute | solution.py:79
  60.8 6.8 %attn_forward.2 = (bf16[512,1024]{1,0:T(8,128)(2,1)S(1)}, f32[512,512]{1,0:T(8,128)S(1)}, bf16[512,768]{1,0:T(8,128)(2,1)S(1)}, f32[512,4]{1,0:T(8,128)S(1)}, bf...) custom-call(s32[2,8]{1,0:T(2,128)S(1)} %fusion.1.table_ref, ...), custom_call_target="tpu_custom_call" | custom-call | flops 1207959552 | bytes 10308672 | tf_op jit(solution)/shard_map/attn_forward/pallas_call | solution.py:66
  69.1 8.5 %collective-permute-start.19 = (bf16[128,1024]{1,0:T(8,128)(2,1)S(1)}, bf16[128,1024]{1,0:T(8,128)(2,1)S(1)}, u32[]{:S(2)}, u32[]{:S(2)}) collective-permute-start(bf16[128,1024]{1,0:T(8,128)(2,1)S(1)} %get-tuple-element.304), channel_id=1, source_target_pairs={{0,2},{2,0},{1,3},{3,1},{4,6},{6,4},{5,7},{7,5},{8,10},{10,8},{9,1... | collective-permute-start | bytes 786440 | tf_op jit(solution)/shard_map/ppermute | solution.py:79
  81.5 3.9 collective-permute-done.35.refs_1_
  88.1 3.8 collective-permute-done.20.refs_2_
  99.7 2.6 collective-permute-done.37.refs_2_
  110.0 6.0 %mlp_forward.2 = (bf16[512,1024]{1,0:T(8,128)(2,1)S(1)}, bf16[512,1024]{1,0:T(8,128)(2,1)S(1)}, bf16[512,1024]{1,0:T(8,128)(2,1)S(1)}, f32[128,1024]{1,0:T(8,128...) custom-call(s32[2,8]{1,0:T(2,128)S(1)} %fusion.1.table_ref, ...), custom_call_target="tpu_custom_call" | custom-call | flops 2147483648 | bytes 17829952 | tf_op jit(solution)/shard_map/mlp_forward/pallas_call | solution.py:66
  128.2 3.0 collective-permute-done.34.refs_2_
  135.7 5.7 %collective-permute-done.43.refs_10_ = bf16[128,1024]{1,0:T(8,128)(2,1)} collective-permute-done((bf16[128,1024]{1,0:T(8,128)(2,1)}, bf16[128,1024]{1,0:T(8,128)(2,1)}, u32[]{:S(2)}, u32[]{:S(2)}) %collective-permute-start.43) | collective-permute-done | bytes 262176 | tf_op jit(solution)/shard_map/ppermute | solution.py:79
  144.7 6.2 %attn_forward.3 = (bf16[512,1024]{1,0:T(8,128)(2,1)S(1)}, f32[512,512]{1,0:T(8,128)S(1)}, bf16[512,768]{1,0:T(8,128)(2,1)S(1)}, f32[512,4]{1,0:T(8,128)S(1)}, bf...) custom-call(s32[2,8]{1,0:T(2,128)S(1)} %fusion.1.table_ref, ...), custom_call_target="tpu_custom_call" | custom-call | flops 1207959552 | bytes 9980992 | tf_op jit(solution)/shard_map/attn_forward/pallas_call | solution.py:66
  151.6 5.2 %collective-permute-done.51.refs_2_.refs_10_ = bf16[256,1024]{1,0:T(8,128)(2,1)} collective-permute-done((bf16[256,1024]{1,0:T(8,128)(2,1)}, bf16[256,1024]{1,0:T(8,128)(2,1)}, u32[]{:S(2)}, u32[]{:S(2)}) %collective-permute-start.51) | collective-permute-done | bytes 524320 | tf_op jit(solution)/shard_map/ppermute | solution.py:272
  161.7 6.9 %collective-permute-done.48.refs_2_ = bf16[128,1024]{1,0:T(8,128)(2,1)S(1)} collective-permute-done((bf16[128,1024]{1,0:T(8,128)(2,1)S(1)}, bf16[128,1024]{1,0:T(8,128)(2,1)S(1)}, u32[]{:S(2)}, u32[]{:S(2)}) %collective-permute-start.48) | collective-permute-done | bytes 262176 | tf_op jit(solution)/shard_map/ppermute | solution.py:79
  172.7 2.9 collective-permute-start.58
  178.9 6.1 %mlp_forward.3 = (bf16[512,1024]{1,0:T(8,128)(2,1)S(1)}, bf16[512,1024]{1,0:T(8,128)(2,1)S(1)}, bf16[512,1024]{1,0:T(8,128)(2,1)S(1)}, f32[128,1024]{1,0:T(8,128...) custom-call(s32[2,8]{1,0:T(2,128)S(1)} %fusion.1.table_ref, ...), custom_call_target="tpu_custom_call" | custom-call | flops 2147483648 | bytes 17829952 | tf_op jit(solution)/shard_map/mlp_forward/pallas_call | solution.py:66
  184.9 3.4 collective-permute-start.61
  189.9 7.3 %collective-permute-done.62.refs_2_ = bf16[128,1024]{1,0:T(8,128)(2,1)S(1)} collective-permute-done((bf16[128,1024]{1,0:T(8,128)(2,1)S(1)}, bf16[128,1024]{1,0:T(8,128)(2,1)S(1)}, u32[]{:S(2)}, u32[]{:S(2)}) %collective-permute-start.62) | collective-permute-done | bytes 262176 | tf_op jit(solution)/shard_map/ppermute | solution.py:79
  199.7 4.9 %collective-permute-done.63.refs_1_ = bf16[128,1024]{1,0:T(8,128)(2,1)S(1)} collective-permute-done((bf16[128,1024]{1,0:T(8,128)(2,1)S(1)}, bf16[128,1024]{1,0:T(8,128)(2,1)S(1)}, u32[]{:S(2)}, u32[]{:S(2)}) %collective-permute-start.63) | collective-permute-done | bytes 262176 | tf_op jit(solution)/shard_map/ppermute | solution.py:79
  207.9 4.0 mlp_backward.2
  212.3 4.6 %mlp_weight_grads.2 = (bf16[128,1024]{1,0:T(8,128)(2,1)}, bf16[256,1024]{1,0:T(8,128)(2,1)}, bf16[256,1024]{1,0:T(8,128)(2,1)}, bf16[256,1024]{1,0:T(8,128)(2,1)...) custom-call(s32[2,8]{1,0:T(2,128)S(1)} %fusion.1.table_ref, ...), custom_call_target="tpu_custom_call" | custom-call | flops 2147483648 | bytes 8388672 | tf_op jit(solution)/shard_map/mlp_weight_grads/pallas_call | solution.py:66
  220.0 5.9 %collective-permute-done.68.refs_6_ = bf16[128,1024]{1,0:T(8,128)(2,1)S(1)} collective-permute-done((bf16[128,1024]{1,0:T(8,128)(2,1)S(1)}, bf16[128,1024]{1,0:T(8,128)(2,1)S(1)}, u32[]{:S(2)}, u32[]{:S(2)}) %collective-permute-start.68) | collective-permute-done | bytes 262176 | tf_op jit(solution)/shard_map/ppermute | solution.py:79
  229.7 3.5 collective-permute-done.69.refs_1_
  236.9 7.5 %attn_backward.2 = (bf16[512,1024]{1,0:T(8,128)(2,1)S(1)}, bf16[512,768]{1,0:T(8,128)(2,1)S(1)}, f32[1,768]{1,0:T(1,128)S(1)}, f32[4,256]{1,0:T(4,128)S(1)}, f32...) custom-call(bf16[128,1024]{1,0:T(8,128)(2,1)S(1)} %get-tuple-element, ...), custom_call_target="tpu_custom_call" | custom-call | flops 1409286144 | bytes 8410112 | tf_op jit(solution)/shard_map/attn_backward/pallas_call | solution.py:66
  245.1 3.8 collective-permute-done.74.refs_0_
  249.1 3.2 attn_weight_grads.2
  258.3 6.9 %collective-permute-done.78.refs_6_ = bf16[128,1024]{1,0:T(8,128)(2,1)S(1)} collective-permute-done((bf16[128,1024]{1,0:T(8,128)(2,1)S(1)}, bf16[128,1024]{1,0:T(8,128)(2,1)S(1)}, u32[]{:S(2)}, u32[]{:S(2)}) %collective-permute-start.78) | collective-permute-done | bytes 262176 | tf_op jit(solution)/shard_map/ppermute | solution.py:79
  266.2 2.9 collective-permute-done.80.refs_0_
  272.6 2.9 collective-permute-start.82
  277.0 3.9 mlp_backward.3
  281.5 4.6 %mlp_weight_grads.3 = (bf16[128,1024]{1,0:T(8,128)(2,1)}, bf16[256,1024]{1,0:T(8,128)(2,1)}, bf16[256,1024]{1,0:T(8,128)(2,1)}, bf16[256,1024]{1,0:T(8,128)(2,1)...) custom-call(s32[2,8]{1,0:T(2,128)S(1)} %fusion.1.table_ref, ...), custom_call_target="tpu_custom_call" | custom-call | flops 2147483648 | bytes 8388672 | tf_op jit(solution)/shard_map/mlp_weight_grads/pallas_call | solution.py:66
  293.2 4.4 %collective-permute-start.87 = (bf16[32,1024]{1,0:T(8,128)(2,1)S(1)}, bf16[32,1024]{1,0:T(8,128)(2,1)S(1)}, u32[]{:S(2)}, u32[]{:S(2)}) collective-permute-start(bf16[32,1024]{1,0:T(8,128)(2,1)S(1)} %get-tuple-element.441), channel_id=1, source_target_pairs={{0,2},{2,0},{1,3},{3,1},{4,6},{6,4},{5,7},{7,5},{8,10},{10,8},{9,1... | collective-permute-start | bytes 196616 | tf_op jit(solution)/shard_map/ppermute | solution.py:79
  299.1 3.1 collective-permute-done.88.refs_15_
  302.6 2.5 collective-permute-done.91.refs_6_
  310.3 4.1 collective-permute-start.95
  316.7 7.9 %attn_backward.3 = (bf16[512,1024]{1,0:T(8,128)(2,1)S(1)}, bf16[512,768]{1,0:T(8,128)(2,1)S(1)}, f32[1,768]{1,0:T(1,128)S(1)}, f32[4,256]{1,0:T(4,128)S(1)}, f32...) custom-call(bf16[128,1024]{1,0:T(8,128)(2,1)S(1)} %get-tuple-element., ...), custom_call_target="tpu_custom_call" | custom-call | flops 1409286144 | bytes 8410112 | tf_op jit(solution)/shard_map/attn_backward/pallas_call | solution.py:66
  326.1 3.3 attn_weight_grads.3
  340.5 2.6 collective-permute-done.104.refs_5_
  348.3 3.1 collective-permute-done.122
  353.7 2.6 collective-permute-done.123
  356.6 13.8 %collective-permute-done.124 = f32[11776]{0:T(1024)S(1)} collective-permute-done((f32[11776]{0:T(1024)S(1)}, f32[11776]{0:T(1024)S(1)}, u32[]{:S(2)}, u32[]{:S(2)}) %collective-permute-start.124) | collective-permute-done | bytes 47136 | tf_op jit(solution)/shard_map/ppermute | solution.py:497
  375.8 6.4 %collective-permute-start.120 = (bf16[32,1024]{1,0:T(8,128)(2,1)}, bf16[32,1024]{1,0:T(8,128)(2,1)S(1)}, u32[]{:S(2)}, u32[]{:S(2)}) collective-permute-start(bf16[32,1024]{1,0:T(8,128)(2,1)} %bitcast.28), channel_id=1, source_target_pairs={{0,0},{4,1},{8,2},{12,3},{16,4},{20,5},{24,6},{28,7},{1,8},{5,9},{... | collective-permute-start | bytes 196616 | tf_op jit(solution)/shard_map/ppermute | solution.py:1183
  382.2 9.0 %collective-permute-done.125 = f32[9472]{0:T(1024)S(1)} collective-permute-done((f32[9472]{0:T(1024)S(1)}, f32[9472]{0:T(1024)S(1)}, u32[]{:S(2)}, u32[]{:S(2)}) %collective-permute-start.125) | collective-permute-done | bytes 37920 | tf_op jit(solution)/shard_map/ppermute | solution.py:497
  395.3 2.9 collective-permute-done.109.refs_0_
  404.5 5.2 %collective-permute-start.117 = (bf16[32,1024]{1,0:T(8,128)(2,1)S(1)}, bf16[32,1024]{1,0:T(8,128)(2,1)S(1)}, u32[]{:S(2)}, u32[]{:S(2)}) collective-permute-start(bf16[32,1024]{1,0:T(8,128)(2,1)S(1)} %get-tuple-element.522), channel_id=1, source_target_pairs={{0,2},{2,0},{1,3},{3,1},{4,6},{6,4},{5,7},{7,5},{8,10},{10,8},{9,1... | collective-permute-start | bytes 196616 | tf_op jit(solution)/shard_map/ppermute | solution.py:79
  412.8 4.3 %collective-permute-start.119 = (bf16[32,1024]{1,0:T(8,128)(2,1)S(1)}, bf16[32,1024]{1,0:T(8,128)(2,1)S(1)}, u32[]{:S(2)}, u32[]{:S(2)}) collective-permute-start(bf16[32,1024]{1,0:T(8,128)(2,1)S(1)} %bitcast.56), channel_id=1, source_target_pairs={{0,0},{4,1},{8,2},{12,3},{16,4},{20,5},{24,6},{28,7},{1,8},{5,9},{... | collective-permute-start | bytes 196616 | tf_op jit(solution)/shard_map/ppermute | solution.py:1183
  (559 shorter events, 186.9 us)
Async XLA Ops:
  3.8 12.6 %collective-permute-start = (bf16[48,1792]{1,0:T(8,128)(2,1)S(1)}, bf16[48,1792]{1,0:T(8,128)(2,1)S(1)}, u32[]{:S(2)}, u32[]{:S(2)}) collective-permute-start(bf16[48,1792]{1,0:T(8,128)(2,1)S(1)} %get-tuple-element.279), channel_id=1, source_target_pairs={{0,1},{1,0},{2,3},{3,2},{4,5},{5,4},{6,7},{7,6},{8,9},{9,8},{10,11... | collective-permute-start | bytes 516104 | tf_op jit(solution)/shard_map/ppermute | solution.py:79
  4.1 12.3 %collective-permute-start.1 = (bf16[48,1792]{1,0:T(8,128)(2,1)S(1)}, bf16[48,1792]{1,0:T(8,128)(2,1)S(1)}, u32[]{:S(2)}, u32[]{:S(2)}) collective-permute-start(bf16[48,1792]{1,0:T(8,128)(2,1)S(1)} %get-tuple-element.280), channel_id=1, source_target_pairs={{0,2},{2,0},{1,3},{3,1},{4,6},{6,4},{5,7},{7,5},{8,10},{10,8},{9,1... | collective-permute-start | bytes 516104 | tf_op jit(solution)/shard_map/ppermute | solution.py:79
  5.1 11.3 %collective-permute-start.2 = (bf16[48,1792]{1,0:T(8,128)(2,1)S(1)}, bf16[48,1792]{1,0:T(8,128)(2,1)S(1)}, u32[]{:S(2)}, u32[]{:S(2)}) collective-permute-start(bf16[48,1792]{1,0:T(8,128)(2,1)S(1)} %get-tuple-element.281), channel_id=1, source_target_pairs={{0,3},{1,2},{2,1},{3,0},{4,7},{5,6},{6,5},{7,4},{8,11},{9,10},{10,... | collective-permute-start | bytes 516104 | tf_op jit(solution)/shard_map/ppermute | solution.py:83
  6.2 10.2 %collective-permute-start.3 = (bf16[2,32,1024]{2,1,0:T(8,128)(2,1)}, bf16[2,32,1024]{2,1,0:T(8,128)(2,1)S(1)}, u32[]{:S(2)}, u32[]{:S(2)}) collective-permute-start(bf16[2,32,1024]{2,1,0:T(8,128)(2,1)} %param.22), channel_id=1, source_target_pairs={{0,0},{1,4},{2,8},{3,12},{4,16},{5,20},{6,24},{7,28},{8,1},{9,5},{... | collective-permute-start | bytes 393224 | tf_op jit(solution)/shard_map/ppermute | solution.py:1051
  29.0 20.0 %collective-permute-start.15 = (bf16[128,1024]{1,0:T(8,128)(2,1)S(1)}, bf16[128,1024]{1,0:T(8,128)(2,1)}, u32[]{:S(2)}, u32[]{:S(2)}) collective-permute-start(bf16[128,1024]{1,0:T(8,128)(2,1)S(1)} %copy-done.13), channel_id=1, source_target_pairs={{0,1},{1,0},{2,3},{3,2},{4,5},{5,4},{6,7},{7,6},{8,9},{9,8},{10,11... | collective-permute-start | bytes 786440 | tf_op jit(solution)/shard_map/ppermute | solution.py:79
  30.7 28.4 %collective-permute-start.16 = (bf16[128,1024]{1,0:T(8,128)(2,1)S(1)}, bf16[128,1024]{1,0:T(8,128)(2,1)}, u32[]{:S(2)}, u32[]{:S(2)}) collective-permute-start(bf16[128,1024]{1,0:T(8,128)(2,1)S(1)} %copy-done.13), channel_id=1, source_target_pairs={{0,2},{2,0},{1,3},{3,1},{4,6},{6,4},{5,7},{7,5},{8,10},{10,8},{9,1... | collective-permute-start | bytes 786440 | tf_op jit(solution)/shard_map/ppermute | solution.py:79
  47.4 10.2 %collective-permute-start.21 = (bf16[256,1024]{1,0:T(8,128)(2,1)S(1)}, bf16[256,1024]{1,0:T(8,128)(2,1)}, u32[]{:S(2)}, u32[]{:S(2)}) collective-permute-start(bf16[256,1024]{1,0:T(8,128)(2,1)S(1)} %get-tuple-element.307.refs_0_.refs_8_), channel_id=1, source_target_pairs={{4,12},{12,20},{20,28},{28,24},{24,16},{16,8},{8,0},{0,4},{5,13},{... | collective-permute-start | bytes 1572872 | tf_op jit(solution)/shard_map/ppermute | solution.py:272
  49.0 10.2 %collective-permute-start.17 = (bf16[128,1024]{1,0:T(8,128)(2,1)}, bf16[128,1024]{1,0:T(8,128)(2,1)S(1)}, u32[]{:S(2)}, u32[]{:S(2)}) collective-permute-start(bf16[128,1024]{1,0:T(8,128)(2,1)} %collective-permute-done.15.refs_10_), channel_id=1, source_target_pairs={{0,2},{2,0},{1,3},{3,1},{4,6},{6,4},{5,7},{7,5},{8,10},{10,8},{9,1... | collective-permute-start | bytes 786440 | tf_op jit(solution)/shard_map/ppermute | solution.py:79
  57.7 21.6 %collective-permute-start.23 = (bf16[256,1024]{1,0:T(8,128)(2,1)}, bf16[256,1024]{1,0:T(8,128)(2,1)S(1)}, u32[]{:S(2)}, u32[]{:S(2)}) collective-permute-start(bf16[256,1024]{1,0:T(8,128)(2,1)} %collective-permute-done.21.refs_1_.refs_9_), channel_id=1, source_target_pairs={{4,12},{12,20},{20,28},{28,24},{24,16},{16,8},{8,0},{0,4},{5,13},{... | collective-permute-start | bytes 1572872 | tf_op jit(solution)/shard_map/ppermute | solution.py:272
  58.4 21.3 %collective-permute-start.24 = (bf16[256,1024]{1,0:T(8,128)(2,1)}, bf16[256,1024]{1,0:T(8,128)(2,1)S(1)}, u32[]{:S(2)}, u32[]{:S(2)}) collective-permute-start(bf16[256,1024]{1,0:T(8,128)(2,1)} %collective-permute-done.22.refs_4_.refs_12_), channel_id=1, source_target_pairs={{4,0},{12,4},{20,12},{28,20},{24,28},{16,24},{8,16},{0,8},{5,1},{1... | collective-permute-start | bytes 1572872 | tf_op jit(solution)/shard_map/ppermute | solution.py:272
  69.1 12.3 %collective-permute-start.19 = (bf16[128,1024]{1,0:T(8,128)(2,1)S(1)}, bf16[128,1024]{1,0:T(8,128)(2,1)S(1)}, u32[]{:S(2)}, u32[]{:S(2)}) collective-permute-start(bf16[128,1024]{1,0:T(8,128)(2,1)S(1)} %get-tuple-element.304), channel_id=1, source_target_pairs={{0,2},{2,0},{1,3},{3,1},{4,6},{6,4},{5,7},{7,5},{8,10},{10,8},{9,1... | collective-permute-start | bytes 786440 | tf_op jit(solution)/shard_map/ppermute | solution.py:79
  79.7 16.9 %collective-permute-start.25 = (bf16[256,1024]{1,0:T(8,128)(2,1)S(1)}, bf16[256,1024]{1,0:T(8,128)(2,1)S(1)}, u32[]{:S(2)}, u32[]{:S(2)}) collective-permute-start(bf16[256,1024]{1,0:T(8,128)(2,1)S(1)} %collective-permute-done.23.refs_2_.refs_10_), channel_id=1, source_target_pairs={{4,12},{12,20},{20,28},{28,24},{24,16},{16,8},{8,0},{0,4},{5,13},{... | collective-permute-start | bytes 1572872 | tf_op jit(solution)/shard_map/ppermute | solution.py:272
  81.4 16.7 %collective-permute-start.26 = (bf16[256,1024]{1,0:T(8,128)(2,1)S(1)}, bf16[256,1024]{1,0:T(8,128)(2,1)S(1)}, u32[]{:S(2)}, u32[]{:S(2)}) collective-permute-start(bf16[256,1024]{1,0:T(8,128)(2,1)S(1)} %collective-permute-done.24.refs_5_.refs_13_), channel_id=1, source_target_pairs={{4,0},{12,4},{20,12},{28,20},{24,28},{16,24},{8,16},{0,8},{5,1},{1... | collective-permute-start | bytes 1572872 | tf_op jit(solution)/shard_map/ppermute | solution.py:272
  86.8 15.4 %collective-permute-start.37 = (bf16[128,1024]{1,0:T(8,128)(2,1)S(1)}, bf16[128,1024]{1,0:T(8,128)(2,1)S(1)}, u32[]{:S(2)}, u32[]{:S(2)}) collective-permute-start(bf16[128,1024]{1,0:T(8,128)(2,1)S(1)} %collective-permute-done.35.refs_1_), channel_id=1, source_target_pairs={{4,12},{12,20},{20,28},{28,24},{24,16},{16,8},{8,0},{0,4},{5,13},{... | collective-permute-start | bytes 786440 | tf_op jit(solution)/shard_map/ppermute | solution.py:272
  92.3 11.3 %collective-permute-start.29 = (bf16[128,1024]{1,0:T(8,128)(2,1)S(1)}, bf16[128,1024]{1,0:T(8,128)(2,1)S(1)}, u32[]{:S(2)}, u32[]{:S(2)}) collective-permute-start(bf16[128,1024]{1,0:T(8,128)(2,1)S(1)} %get-tuple-element.316.refs_16_), channel_id=1, source_target_pairs={{0,1},{1,0},{2,3},{3,2},{4,5},{5,4},{6,7},{7,6},{8,9},{9,8},{10,11... | collective-permute-start | bytes 786440 | tf_op jit(solution)/shard_map/ppermute | solution.py:79
  92.9 10.8 %collective-permute-start.38 = (bf16[128,1024]{1,0:T(8,128)(2,1)S(1)}, bf16[128,1024]{1,0:T(8,128)(2,1)S(1)}, u32[]{:S(2)}, u32[]{:S(2)}) collective-permute-start(bf16[128,1024]{1,0:T(8,128)(2,1)S(1)} %collective-permute-done.36.refs_4_), channel_id=1, source_target_pairs={{4,0},{12,4},{20,12},{28,20},{24,28},{16,24},{8,16},{0,8},{5,1},{1... | collective-permute-start | bytes 786440 | tf_op jit(solution)/shard_map/ppermute | solution.py:272
  103.7 17.2 %collective-permute-start.39 = (bf16[128,1024]{1,0:T(8,128)(2,1)S(1)}, bf16[128,1024]{1,0:T(8,128)(2,1)S(1)}, u32[]{:S(2)}, u32[]{:S(2)}) collective-permute-start(bf16[128,1024]{1,0:T(8,128)(2,1)S(1)} %collective-permute-done.37.refs_2_), channel_id=1, source_target_pairs={{4,12},{12,20},{20,28},{28,24},{24,16},{16,8},{8,0},{0,4},{5,13},{... | collective-permute-start | bytes 786440 | tf_op jit(solution)/shard_map/ppermute | solution.py:272
  107.8 13.1 %collective-permute-start.40 = (bf16[128,1024]{1,0:T(8,128)(2,1)S(1)}, bf16[128,1024]{1,0:T(8,128)(2,1)S(1)}, u32[]{:S(2)}, u32[]{:S(2)}) collective-permute-start(bf16[128,1024]{1,0:T(8,128)(2,1)S(1)} %collective-permute-done.38.refs_5_), channel_id=1, source_target_pairs={{4,0},{12,4},{20,12},{28,20},{24,28},{16,24},{8,16},{0,8},{5,1},{1... | collective-permute-start | bytes 786440 | tf_op jit(solution)/shard_map/ppermute | solution.py:272
  126.8 16.2 %collective-permute-start.49 = (bf16[256,1024]{1,0:T(8,128)(2,1)S(1)}, bf16[256,1024]{1,0:T(8,128)(2,1)}, u32[]{:S(2)}, u32[]{:S(2)}) collective-permute-start(bf16[256,1024]{1,0:T(8,128)(2,1)S(1)} %get-tuple-element.337.refs_0_.refs_8_), channel_id=1, source_target_pairs={{4,12},{12,20},{20,28},{28,24},{24,16},{16,8},{8,0},{0,4},{5,13},{... | collective-permute-start | bytes 1572872 | tf_op jit(solution)/shard_map/ppermute | solution.py:272
  127.9 15.1 %collective-permute-start.50 = (bf16[256,1024]{1,0:T(8,128)(2,1)S(1)}, bf16[256,1024]{1,0:T(8,128)(2,1)}, u32[]{:S(2)}, u32[]{:S(2)}) collective-permute-start(bf16[256,1024]{1,0:T(8,128)(2,1)S(1)} %get-tuple-element.337.refs_0_.refs_8_), channel_id=1, source_target_pairs={{4,0},{12,4},{20,12},{28,20},{24,28},{16,24},{8,16},{0,8},{5,1},{1... | collective-permute-start | bytes 1572872 | tf_op jit(solution)/shard_map/ppermute | solution.py:272
  143.0 13.8 %collective-permute-start.51 = (bf16[256,1024]{1,0:T(8,128)(2,1)}, bf16[256,1024]{1,0:T(8,128)(2,1)}, u32[]{:S(2)}, u32[]{:S(2)}) collective-permute-start(bf16[256,1024]{1,0:T(8,128)(2,1)} %collective-permute-done.49.refs_1_.refs_9_), channel_id=1, source_target_pairs={{4,12},{12,20},{20,28},{28,24},{24,16},{16,8},{8,0},{0,4},{5,13},{... | collective-permute-start | bytes 1572872 | tf_op jit(solution)/shard_map/ppermute | solution.py:272
  143.8 13.5 %collective-permute-start.52 = (bf16[256,1024]{1,0:T(8,128)(2,1)}, bf16[256,1024]{1,0:T(8,128)(2,1)}, u32[]{:S(2)}, u32[]{:S(2)}) collective-permute-start(bf16[256,1024]{1,0:T(8,128)(2,1)} %collective-permute-done.50.refs_4_.refs_12_), channel_id=1, source_target_pairs={{4,0},{12,4},{20,12},{28,20},{24,28},{16,24},{8,16},{0,8},{5,1},{1... | collective-permute-start | bytes 1572872 | tf_op jit(solution)/shard_map/ppermute | solution.py:272
  157.3 12.5 %collective-permute-start.53 = (bf16[256,1024]{1,0:T(8,128)(2,1)}, bf16[256,1024]{1,0:T(8,128)(2,1)S(1)}, u32[]{:S(2)}, u32[]{:S(2)}) collective-permute-start(bf16[256,1024]{1,0:T(8,128)(2,1)} %collective-permute-done.51.refs_2_.refs_10_), channel_id=1, source_target_pairs={{4,12},{12,20},{20,28},{28,24},{24,16},{16,8},{8,0},{0,4},{5,13},{... | collective-permute-start | bytes 1572872 | tf_op jit(solution)/shard_map/ppermute | solution.py:272
  158.5 12.2 %collective-permute-start.54 = (bf16[256,1024]{1,0:T(8,128)(2,1)}, bf16[256,1024]{1,0:T(8,128)(2,1)S(1)}, u32[]{:S(2)}, u32[]{:S(2)}) collective-permute-start(bf16[256,1024]{1,0:T(8,128)(2,1)} %collective-permute-done.52.refs_5_.refs_13_), channel_id=1, source_target_pairs={{4,0},{12,4},{20,12},{28,20},{24,28},{16,24},{8,16},{0,8},{5,1},{1... | collective-permute-start | bytes 1572872 | tf_op jit(solution)/shard_map/ppermute | solution.py:272
  235.3 13.6 %collective-permute-start.74 = (bf16[256,1024]{1,0:T(8,128)(2,1)S(1)}, bf16[256,1024]{1,0:T(8,128)(2,1)S(1)}, u32[]{:S(2)}, u32[]{:S(2)}) collective-permute-start(bf16[256,1024]{1,0:T(8,128)(2,1)S(1)} %get-tuple-element.380), channel_id=1, source_target_pairs={{4,12},{12,20},{20,28},{28,24},{24,16},{16,8},{8,0},{0,4},{5,13},{... | collective-permute-start | bytes 1572872 | tf_op jit(solution)/shard_map/ppermute | solution.py:272
  235.7 13.4 %collective-permute-start.75 = (bf16[256,1024]{1,0:T(8,128)(2,1)S(1)}, bf16[256,1024]{1,0:T(8,128)(2,1)S(1)}, u32[]{:S(2)}, u32[]{:S(2)}) collective-permute-start(bf16[256,1024]{1,0:T(8,128)(2,1)S(1)} %get-tuple-element.381), channel_id=1, source_target_pairs={{4,0},{12,4},{20,12},{28,20},{24,28},{16,24},{8,16},{0,8},{5,1},{1... | collective-permute-start | bytes 1572872 | tf_op jit(solution)/shard_map/ppermute | solution.py:272
  244.5 12.7 %collective-permute-start.77 = (bf16[128,1024]{1,0:T(8,128)(2,1)S(1)}, bf16[128,1024]{1,0:T(8,128)(2,1)S(1)}, u32[]{:S(2)}, u32[]{:S(2)}) collective-permute-start(bf16[128,1024]{1,0:T(8,128)(2,1)S(1)} %get-tuple-element.406), channel_id=1, source_target_pairs={{0,2},{2,0},{1,3},{3,1},{4,6},{6,4},{5,7},{7,5},{8,10},{10,8},{9,1... | collective-permute-start | bytes 786440 | tf_op jit(solution)/shard_map/ppermute | solution.py:79
  254.0 15.2 %collective-permute-start.80 = (bf16[320,1024]{1,0:T(8,128)(2,1)S(1)}, bf16[320,1024]{1,0:T(8,128)(2,1)S(1)}, u32[]{:S(2)}, u32[]{:S(2)}) collective-permute-start(bf16[320,1024]{1,0:T(8,128)(2,1)S(1)} %get-tuple-element.402), channel_id=1, source_target_pairs={{4,12},{12,20},{20,28},{28,24},{24,16},{16,8},{8,0},{0,4},{5,13},{... | collective-permute-start | bytes 1966088 | tf_op jit(solution)/shard_map/ppermute | solution.py:272
  254.3 14.8 %collective-permute-start.81 = (bf16[320,1024]{1,0:T(8,128)(2,1)S(1)}, bf16[320,1024]{1,0:T(8,128)(2,1)S(1)}, u32[]{:S(2)}, u32[]{:S(2)}) collective-permute-start(bf16[320,1024]{1,0:T(8,128)(2,1)S(1)} %get-tuple-element.403), channel_id=1, source_target_pairs={{4,0},{12,4},{20,12},{28,20},{24,28},{16,24},{8,16},{0,8},{5,1},{1... | collective-permute-start | bytes 1966088 | tf_op jit(solution)/shard_map/ppermute | solution.py:272
  270.9 16.8 %collective-permute-start.84 = (bf16[384,1024]{1,0:T(8,128)(2,1)S(1)}, bf16[384,1024]{1,0:T(8,128)(2,1)S(1)}, u32[]{:S(2)}, u32[]{:S(2)}) collective-permute-start(bf16[384,1024]{1,0:T(8,128)(2,1)S(1)} %get-tuple-element.418), channel_id=1, source_target_pairs={{4,12},{12,20},{20,28},{28,24},{24,16},{16,8},{8,0},{0,4},{5,13},{... | collective-permute-start | bytes 2359304 | tf_op jit(solution)/shard_map/ppermute | solution.py:272
  271.9 16.6 %collective-permute-start.85 = (bf16[384,1024]{1,0:T(8,128)(2,1)S(1)}, bf16[384,1024]{1,0:T(8,128)(2,1)S(1)}, u32[]{:S(2)}, u32[]{:S(2)}) collective-permute-start(bf16[384,1024]{1,0:T(8,128)(2,1)S(1)} %get-tuple-element.419), channel_id=1, source_target_pairs={{4,0},{12,4},{20,12},{28,20},{24,28},{16,24},{8,16},{0,8},{5,1},{1... | collective-permute-start | bytes 2359304 | tf_op jit(solution)/shard_map/ppermute | solution.py:272
  281.0 16.6 %collective-permute-start.90 = (bf16[128,1024]{1,0:T(8,128)(2,1)S(1)}, bf16[128,1024]{1,0:T(8,128)(2,1)S(1)}, u32[]{:S(2)}, u32[]{:S(2)}) collective-permute-start(bf16[128,1024]{1,0:T(8,128)(2,1)S(1)} %get-tuple-element.447), channel_id=1, source_target_pairs={{0,2},{2,0},{1,3},{3,1},{4,6},{6,4},{5,7},{7,5},{8,10},{10,8},{9,1... | collective-permute-start | bytes 786440 | tf_op jit(solution)/shard_map/ppermute | solution.py:79
  290.3 14.8 %collective-permute-start.92 = (bf16[256,1024]{1,0:T(8,128)(2,1)S(1)}, bf16[256,1024]{1,0:T(8,128)(2,1)S(1)}, u32[]{:S(2)}, u32[]{:S(2)}) collective-permute-start(bf16[256,1024]{1,0:T(8,128)(2,1)S(1)} %get-tuple-element.443), channel_id=1, source_target_pairs={{4,12},{12,20},{20,28},{28,24},{24,16},{16,8},{8,0},{0,4},{5,13},{... | collective-permute-start | bytes 1572872 | tf_op jit(solution)/shard_map/ppermute | solution.py:272
  290.8 14.3 %collective-permute-start.93 = (bf16[256,1024]{1,0:T(8,128)(2,1)S(1)}, bf16[256,1024]{1,0:T(8,128)(2,1)S(1)}, u32[]{:S(2)}, u32[]{:S(2)}) collective-permute-start(bf16[256,1024]{1,0:T(8,128)(2,1)S(1)} %get-tuple-element.444), channel_id=1, source_target_pairs={{4,0},{12,4},{20,12},{28,20},{24,28},{16,24},{8,16},{0,8},{5,1},{1... | collective-permute-start | bytes 1572872 | tf_op jit(solution)/shard_map/ppermute | solution.py:272
  308.5 20.8 %collective-permute-start.97 = (bf16[384,1024]{1,0:T(8,128)(2,1)S(1)}, bf16[384,1024]{1,0:T(8,128)(2,1)S(1)}, u32[]{:S(2)}, u32[]{:S(2)}) collective-permute-start(bf16[384,1024]{1,0:T(8,128)(2,1)S(1)} %get-tuple-element.457), channel_id=1, source_target_pairs={{4,12},{12,20},{20,28},{28,24},{24,16},{16,8},{8,0},{0,4},{5,13},{... | collective-permute-start | bytes 2359304 | tf_op jit(solution)/shard_map/ppermute | solution.py:272
  309.0 20.4 %collective-permute-start.98 = (bf16[384,1024]{1,0:T(8,128)(2,1)S(1)}, bf16[384,1024]{1,0:T(8,128)(2,1)S(1)}, u32[]{:S(2)}, u32[]{:S(2)}) collective-permute-start(bf16[384,1024]{1,0:T(8,128)(2,1)S(1)} %get-tuple-element.458), channel_id=1, source_target_pairs={{4,0},{12,4},{20,12},{28,20},{24,28},{16,24},{8,16},{0,8},{5,1},{1... | collective-permute-start | bytes 2359304 | tf_op jit(solution)/shard_map/ppermute | solution.py:272
  351.9 18.6 %collective-permute-start.105 = (bf16[320,1024]{1,0:T(8,128)(2,1)}, bf16[320,1024]{1,0:T(8,128)(2,1)S(1)}, u32[]{:S(2)}, u32[]{:S(2)}) collective-permute-start(bf16[320,1024]{1,0:T(8,128)(2,1)} %copy-done.71), channel_id=1, source_target_pairs={{4,12},{12,20},{20,28},{28,24},{24,16},{16,8},{8,0},{0,4},{5,13},{... | collective-permute-start | bytes 1966088 | tf_op jit(solution)/shard_map/ppermute | solution.py:272
  352.9 17.6 %collective-permute-start.106 = (bf16[320,1024]{1,0:T(8,128)(2,1)S(1)}, bf16[320,1024]{1,0:T(8,128)(2,1)S(1)}, u32[]{:S(2)}, u32[]{:S(2)}) collective-permute-start(bf16[320,1024]{1,0:T(8,128)(2,1)S(1)} %get-tuple-element.485), channel_id=1, source_target_pairs={{4,0},{12,4},{20,12},{28,20},{24,28},{16,24},{8,16},{0,8},{5,1},{1... | collective-permute-start | bytes 1966088 | tf_op jit(solution)/shard_map/ppermute | solution.py:272
  356.5 13.9 %collective-permute-start.124 = (f32[11776]{0:T(1024)S(1)}, f32[11776]{0:T(1024)S(1)}, u32[]{:S(2)}, u32[]{:S(2)}) collective-permute-start(f32[11776]{0:T(1024)S(1)} %pad_maximum_fusion.4), channel_id=1, source_target_pairs={{0,8},{8,0},{16,24},{24,16},{1,9},{9,1},{17,25},{25,17},{2,10},{10... | collective-permute-start | bytes 141320 | tf_op jit(solution)/shard_map/ppermute | solution.py:497
  372.9 18.3 %collective-permute-start.107 = (bf16[384,1024]{1,0:T(8,128)(2,1)}, bf16[384,1024]{1,0:T(8,128)(2,1)S(1)}, u32[]{:S(2)}, u32[]{:S(2)}) collective-permute-start(bf16[384,1024]{1,0:T(8,128)(2,1)} %get-tuple-element.496), channel_id=1, source_target_pairs={{4,12},{12,20},{20,28},{28,24},{24,16},{16,8},{8,0},{0,4},{5,13},{... | collective-permute-start | bytes 2359304 | tf_op jit(solution)/shard_map/ppermute | solution.py:272
  373.9 17.5 %collective-permute-start.108 = (bf16[384,1024]{1,0:T(8,128)(2,1)S(1)}, bf16[384,1024]{1,0:T(8,128)(2,1)S(1)}, u32[]{:S(2)}, u32[]{:S(2)}) collective-permute-start(bf16[384,1024]{1,0:T(8,128)(2,1)S(1)} %get-tuple-element.497), channel_id=1, source_target_pairs={{4,0},{12,4},{20,12},{28,20},{24,28},{16,24},{8,16},{0,8},{5,1},{1... | collective-permute-start | bytes 2359304 | tf_op jit(solution)/shard_map/ppermute | solution.py:272
  374.5 16.7 %collective-permute-start.125 = (f32[9472]{0:T(1024)S(1)}, f32[9472]{0:T(1024)S(1)}, u32[]{:S(2)}, u32[]{:S(2)}) collective-permute-start(f32[9472]{0:T(1024)S(1)} %pad_maximum_fusion.5), channel_id=1, source_target_pairs={{0,4},{4,0},{1,5},{5,1},{2,6},{6,2},{3,7},{7,3},{8,12},{12,8},{9,1... | collective-permute-start | bytes 113672 | tf_op jit(solution)/shard_map/ppermute | solution.py:497
  375.8 41.4 %collective-permute-start.120 = (bf16[32,1024]{1,0:T(8,128)(2,1)}, bf16[32,1024]{1,0:T(8,128)(2,1)S(1)}, u32[]{:S(2)}, u32[]{:S(2)}) collective-permute-start(bf16[32,1024]{1,0:T(8,128)(2,1)} %bitcast.28), channel_id=1, source_target_pairs={{0,0},{4,1},{8,2},{12,3},{16,4},{20,5},{24,6},{28,7},{1,8},{5,9},{... | collective-permute-start | bytes 196616 | tf_op jit(solution)/shard_map/ppermute | solution.py:1183
  400.3 11.2 %collective-permute-start.112 = (bf16[128,1024]{1,0:T(8,128)(2,1)S(1)}, bf16[128,1024]{1,0:T(8,128)(2,1)S(1)}, u32[]{:S(2)}, u32[]{:S(2)}) collective-permute-start(bf16[128,1024]{1,0:T(8,128)(2,1)S(1)} %get-tuple-element.509), channel_id=1, source_target_pairs={{4,0},{12,4},{20,12},{28,20},{24,28},{16,24},{8,16},{0,8},{5,1},{1... | collective-permute-start | bytes 786440 | tf_op jit(solution)/shard_map/ppermute | solution.py:272
  403.7 15.2 %collective-permute-start.116 = (bf16[32,1024]{1,0:T(8,128)(2,1)S(1)}, bf16[32,1024]{1,0:T(8,128)(2,1)S(1)}, u32[]{:S(2)}, u32[]{:S(2)}) collective-permute-start(bf16[32,1024]{1,0:T(8,128)(2,1)S(1)} %get-tuple-element.521), channel_id=1, source_target_pairs={{0,1},{1,0},{2,3},{3,2},{4,5},{5,4},{6,7},{7,6},{8,9},{9,8},{10,11... | collective-permute-start | bytes 196616 | tf_op jit(solution)/shard_map/ppermute | solution.py:79
  404.5 14.4 %collective-permute-start.117 = (bf16[32,1024]{1,0:T(8,128)(2,1)S(1)}, bf16[32,1024]{1,0:T(8,128)(2,1)S(1)}, u32[]{:S(2)}, u32[]{:S(2)}) collective-permute-start(bf16[32,1024]{1,0:T(8,128)(2,1)S(1)} %get-tuple-element.522), channel_id=1, source_target_pairs={{0,2},{2,0},{1,3},{3,1},{4,6},{6,4},{5,7},{7,5},{8,10},{10,8},{9,1... | collective-permute-start | bytes 196616 | tf_op jit(solution)/shard_map/ppermute | solution.py:79
  409.6 11.6 %collective-permute-start.118 = (bf16[32,1024]{1,0:T(8,128)(2,1)S(1)}, bf16[32,1024]{1,0:T(8,128)(2,1)S(1)}, u32[]{:S(2)}, u32[]{:S(2)}) collective-permute-start(bf16[32,1024]{1,0:T(8,128)(2,1)S(1)} %get-tuple-element.523), channel_id=1, source_target_pairs={{0,3},{1,2},{2,1},{3,0},{4,7},{5,6},{6,5},{7,4},{8,11},{9,10},{10,... | collective-permute-start | bytes 196616 | tf_op jit(solution)/shard_map/ppermute | solution.py:83
  412.8 11.2 %collective-permute-start.119 = (bf16[32,1024]{1,0:T(8,128)(2,1)S(1)}, bf16[32,1024]{1,0:T(8,128)(2,1)S(1)}, u32[]{:S(2)}, u32[]{:S(2)}) collective-permute-start(bf16[32,1024]{1,0:T(8,128)(2,1)S(1)} %bitcast.56), channel_id=1, source_target_pairs={{0,0},{4,1},{8,2},{12,3},{16,4},{20,5},{24,6},{28,7},{1,8},{5,9},{... | collective-permute-start | bytes 196616 | tf_op jit(solution)/shard_map/ppermute | solution.py:1183
  (182 other events, 1959.7 us)
